TPU v7x, 256 devices: a whole 4x4x8 slice. The times are simulated.
256 devices in a mesh: dom: 32 (over y, x, core), slab: 8 (over z).
Axes of the slice: x: 4, y: 4, z: 8, core: 2. Of those that a mesh axis runs over, the one named last changes fastest.
Arguments:
- nullspace: float32 [6, 1179648], P(None, ('dom', 'slab')), may hold values from -6 to 6
- owner_device: int32 [1179648], P(('dom', 'slab')), may hold values from 0 to 255, as said below
- local_aggregate: int32 [1179648], P(('dom', 'slab')), may hold values from 0 to 63, as said below
- position: int32 [1179648], P(('dom', 'slab')), may hold values from 0 to 127, as said below
- sent_rows: int32 [256, 256, 18], P(('dom', 'slab')), may hold values from -1 to 4607, as said below
- arrival_slot: int32 [256, 256, 18], P(('dom', 'slab')), may hold values from -1 to 8191, as said below
Outputs:
- prolongator: float32 [6, 1179648], P(None, ('dom', 'slab'))
- padded_prolongator: float32 [6, 2097152], P(None, ('dom', 'slab'))
- coarse_nullspace: float32 [36, 16384], P(None, ('dom', 'slab'))
Inputs may be any that keep to these rules, and one draw needn't show every extreme that they name: `owner_device`: devices are numbered in dom+slab order. A device holds 4608 rows and owns 64 aggregates; the aggregates of one owner hold 4608 rows in all, each 16 to 128 rows, a multiple of 8, and every owner has an aggregate of 128 rows. The aggregate's global number is owner_device * 64 + local_aggregate. `position`: distinct among the rows of one aggregate and below that aggregate's row count. `sent_rows`: entry [p, q, k] is the k-th row of device p (a local row index) whose aggregate device q owns; every row of p owned elsewhere stands exactly once, live entries of [p, q] come first and -1 fills the rest; [p, p] is empty; [p, q] and [q, p] have equally many live entries, at most 18, and some pair has 18. `arrival_slot`: entry [q, p, k] is local_aggregate * 128 + position of the row sent_rows[p, q, k], -1 where that is -1.
All inputs are finite; a program needn't handle non-finite values.
Results may differ from a plain program's by a relative error of at most 0.0003.
Values sent between devices are 32-bit elements; how exact they have to be, the bound alone decides.
No kernel may reach another device: no remote copies, remote signals or barrier semaphores. Data moves between devices by JAX's collectives and lax.ppermute only.
A program may use at most 64 MiB of HBM per device.

v0:
```python
import jax
import jax.numpy as jnp
from jax import lax
from jax.sharding import PartitionSpec as P

PAD = 128
AGG_DEV = 64


def cholesky_upper(gram_terms, mode_count):
    factor_up = [
        [jnp.zeros_like(gram_terms[0][0]) for right_j in range(mode_count)]
        for left_i in range(mode_count)
    ]
    for left_i in range(mode_count):
        pivot_sq = gram_terms[left_i][left_i]
        for inner_k in range(left_i):
            pivot_sq = pivot_sq - factor_up[inner_k][left_i] * factor_up[inner_k][left_i]
        pivot_val = jnp.sqrt(pivot_sq)
        factor_up[left_i][left_i] = pivot_val
        for right_j in range(left_i + 1, mode_count):
            partial_ij = gram_terms[left_i][right_j]
            for inner_k in range(left_i):
                partial_ij = partial_ij - factor_up[inner_k][left_i] * factor_up[inner_k][right_j]
            factor_up[left_i][right_j] = partial_ij / pivot_val
    return factor_up


def invert_upper(factor_up, mode_count):
    inverse = [
        [jnp.zeros_like(factor_up[0][0]) for right_j in range(mode_count)]
        for left_i in range(mode_count)
    ]
    for left_i in range(mode_count):
        inverse[left_i][left_i] = 1.0 / factor_up[left_i][left_i]
        for right_j in range(left_i + 1, mode_count):
            partial_ij = jnp.zeros_like(factor_up[0][0])
            for inner_k in range(left_i, right_j):
                partial_ij = partial_ij + inverse[left_i][inner_k] * factor_up[inner_k][right_j]
            inverse[left_i][right_j] = -partial_ij / factor_up[right_j][right_j]
    return inverse


def apply_inverse(columns, inverse, mode_count):
    results = []
    for right_j in range(mode_count):
        total_j = columns[0] * inverse[0][right_j]
        for left_i in range(1, right_j + 1):
            total_j = total_j + columns[left_i] * inverse[left_i][right_j]
        results.append(total_j)
    return jnp.stack(results)


def gram_of(padded_rows):
    mode_count = padded_rows.shape[0]
    shaped = padded_rows.reshape(mode_count, AGG_DEV, PAD)
    return jnp.einsum("iap,kap->ika", shaped, shaped, precision=lax.Precision.HIGHEST)


def factor_block(padded_rows, gram_sum):
    mode_count = padded_rows.shape[0]
    shaped = padded_rows.reshape(mode_count, AGG_DEV, PAD)
    gram_terms = [
        [gram_sum[left_i, right_j] for right_j in range(mode_count)] for left_i in range(mode_count)
    ]
    factor_up = cholesky_upper(gram_terms, mode_count)
    inverse = invert_upper(factor_up, mode_count)
    widened = [[entry_value[:, None] for entry_value in inverse_row] for inverse_row in inverse]
    padded_q = apply_inverse([shaped[left_i] for left_i in range(mode_count)], widened, mode_count)
    padded_q = padded_q.reshape(mode_count, -1)
    coarse = jnp.stack(
        [
            factor_up[left_i][right_j]
            for left_i in range(mode_count)
            for right_j in range(mode_count)
        ]
    )
    inverse_table = jnp.stack(
        [
            inverse[left_i][right_j]
            for left_i in range(mode_count)
            for right_j in range(left_i, mode_count)
        ]
    )
    return (padded_q, coarse, inverse_table)


def body(nullspace, owner_device, local_aggregate, position, sent_rows, arrival_slot):
    mode_count = nullspace.shape[0]
    row_count = nullspace.shape[1]
    lane_count = sent_rows.shape[2]
    slot_count = AGG_DEV * PAD
    dom_size = lax.axis_size("dom")
    slab_size = lax.axis_size("slab")
    my_index = lax.axis_index("dom") * slab_size + lax.axis_index("slab")
    outgoing = sent_rows.reshape(-1)
    live_out = outgoing >= 0
    picked = jnp.take(nullspace, jnp.where(live_out, outgoing, 0), axis=1)
    picked = picked.reshape(mode_count, dom_size, slab_size, lane_count)
    arrived = lax.all_to_all(
        lax.all_to_all(picked, "dom", split_axis=1, concat_axis=1, tiled=True),
        "slab",
        split_axis=2,
        concat_axis=2,
        tiled=True,
    ).reshape(mode_count, -1)
    arrive_count = arrived.shape[1]
    owned_here = owner_device == my_index
    own_column = local_aggregate * PAD + position
    local_slot = jnp.where(owned_here, own_column, slot_count)
    landing = arrival_slot.reshape(-1)
    live_in = landing >= 0
    landing_safe = jnp.where(live_in, landing, slot_count)
    zero_column = jnp.zeros((mode_count, 1), jnp.float32)
    row_ids = jnp.arange(row_count, dtype=jnp.int32)
    arrive_ids = jnp.arange(arrive_count, dtype=jnp.int32)
    slot_source = jnp.full((slot_count,), row_count + arrive_count, jnp.int32)
    slot_source = slot_source.at[local_slot].set(row_ids, mode="drop")
    slot_source = slot_source.at[landing_safe].set(row_count + arrive_ids, mode="drop")
    padded_rows = jnp.take(
        jnp.concatenate([nullspace, arrived, zero_column], axis=1), slot_source, axis=1
    )
    gram_sum = gram_of(padded_rows)
    padded_q, coarse, inverse_table = factor_block(padded_rows, gram_sum)
    answer = jnp.take(padded_q, jnp.where(live_in, landing, 0), axis=1)
    answer = answer.reshape(mode_count, dom_size, slab_size, lane_count)
    returned = lax.all_to_all(
        lax.all_to_all(answer, "dom", split_axis=1, concat_axis=1, tiled=True),
        "slab",
        split_axis=2,
        concat_axis=2,
        tiled=True,
    ).reshape(mode_count, -1)
    fine_source = jnp.where(owned_here, own_column, slot_count)
    fine_source = fine_source.at[jnp.where(live_out, outgoing, row_count)].set(
        slot_count + 1 + arrive_ids, mode="drop"
    )
    fine = jnp.take(jnp.concatenate([padded_q, zero_column, returned], axis=1), fine_source, axis=1)
    return (fine, padded_q, coarse)


def solution(mesh):
    in_specs = (
        P(None, ("dom", "slab")),
        P(("dom", "slab")),
        P(("dom", "slab")),
        P(("dom", "slab")),
        P(("dom", "slab"), None, None),
        P(("dom", "slab"), None, None),
    )
    out_specs = (P(None, ("dom", "slab")), P(None, ("dom", "slab")), P(None, ("dom", "slab")))
    return jax.shard_map(body, mesh=mesh, in_specs=in_specs, out_specs=out_specs, check_vma=False)
```

profile of v0, /device:TPU:1, one launch (start us, length us, event | category | flops | bytes accessed | tf_op | source)
XLA Modules:
  0.0 226.4 jit_solution(10656323581645655658)
XLA Ops:
  1.8 1.6 copy.223
  3.4 9.3 %gather_fusion = f32[4608,6]{1,0:T(8,128)} fusion(f32[6,4608]{0,1:T(8,128)S(1)} %copy.223, s32[5120]{0:T(1024)S(1)} %pad_clamp_fusion.2), kind=kCustom, calls=%fused_computation | custom fusion | bytes 239616 | tf_op jit(solution)/shard_map/jit(_take)/gather | solution.py:98
  12.7 2.4 %copy.219 = f32[6,4608]{1,0:T(8,128)S(1)} copy(f32[6,4608]{0,1:T(8,128)} %bitcast.207) | data formatting | bytes 221184 | tf_op jit(solution)/shard_map/jit(_take)/gather | solution.py:98
  16.9 2.3 %reshape.2622 = f32[32,1,864]{2,1,0:T(1,128)} reshape(f32[32,6,8,18]{3,2,1,0:T(8,128)} %copy_bitcast_fusion.1) | data formatting | bytes 221184
  19.2 8.6 %all-to-all-start = ((f32[32,1,864]{2,1,0:T(1,128)}), f32[32,1,864]{2,1,0:T(1,128)S(1)}, u32[]{:S(2)}, u32[]{:S(2)}) async-start(f32[32,1,864]{2,1,0:T(1,128)} %reshape.2622), calls=%async_computation | async-start | bytes 229376 | tf_op jit(solution)/shard_map/all_to_all | solution.py:101
  28.3 17.4 %scatter_custom_fusion.1 = s32[8192]{0:T(1024)S(1)} fusion(s32[4608]{0:T(1024)S(1)} %get-tuple-element.110, s32[4608]{0:T(1024)S(1)} %iota.9, s32[]{:T(128)} %constant.56.clone.1), kind=kCustom, calls=%fused_computation.74 | custom fusion | bytes 32772 | tf_op jit(solution)/shard_map/scatter | solution.py:118
  45.7 17.5 %scatter_fusion.1 = s32[8192]{0:T(1024)S(1)} fusion(s32[8192]{0:T(1024)S(1)} %scatter_custom_fusion.1, s32[4608]{0:T(1024)S(1)} %get-tuple-element.49, s32[4608]{0:T(1024)S(1)} %iota_add_fusion), kind=kCustom, calls=%fused_computation.6 | custom fusion | bytes 73728 | tf_op jit(solution)/shard_map/scatter | solution.py:119
  63.3 17.4 %scatter_fusion = s32[4608]{0:T(1024)S(1)} fusion(s32[4608]{0:T(1024)S(1)} %get-tuple-element.111, s32[4608]{0:T(1024)S(1)} %get-tuple-element.46, s32[4608]{0:T(1024)S(1)} %iota_add_fusion.1), kind=kCustom, calls=%fused_computation.4 | custom fusion | bytes 73728 | tf_op jit(solution)/shard_map/scatter | solution.py:135
  82.7 1.3 copy.221
  84.0 1.9 reshape.2624
  85.9 8.2 %all-to-all-start.1 = ((f32[8,1,3456]{2,1,0:T(1,128)}), f32[8,1,3456]{2,1,0:T(1,128)S(1)}, u32[]{:S(2)}, u32[]{:S(2)}) async-start(f32[8,1,3456]{2,1,0:T(1,128)} %reshape.2624), calls=%async_computation.1 | async-start | bytes 221184 | tf_op jit(solution)/shard_map/all_to_all | solution.py:100
  94.1 7.6 %all-to-all-done.1 = f32[8,1,3456]{2,1,0:T(1,128)S(1)} async-done(((f32[8,1,3456]{2,1,0:T(1,128)}), f32[8,1,3456]{2,1,0:T(1,128)S(1)}, u32[]{:S(2)}, u32[]{:S(2)}) %all-to-all-start.1) | async-done | bytes 110624 | tf_op jit(solution)/shard_map/all_to_all | solution.py:100
  102.6 1.0 reshape.2625
  103.7 1.4 copy.222
  105.5 2.1 copy.224
  107.7 7.3 %maximum_maximum_fusion = f32[6,9217]{0,1:T(8,128)} fusion(f32[6,4608]{0,1:T(8,128)} %copy.224, f32[6,4608]{0,1:T(8,128)S(1)} %copy.223, f32[9217]{0:T(1024)S(1)} %pad.2.clone), kind=kLoop, calls=%fused_computation.7 | loop fusion | flops 110604 | bytes 479260 | tf_op jit(solution)/shard_map/concatenate | solution.py:121
  115.0 30.3 %gather_fusion.1 = f32[8192,6]{1,0:T(8,128)} fusion(f32[6,9217]{0,1:T(8,128)} %maximum_maximum_fusion, s32[8192]{0:T(1024)S(1)} %fusion.3), kind=kCustom, calls=%fused_computation.1 | custom fusion | bytes 425984 | tf_op jit(solution)/shard_map/jit(_take)/gather | solution.py:120
  145.3 2.8 %copy.226 = f32[8192,6]{0,1:T(8,128)S(1)} copy(f32[8192,6]{1,0:T(8,128)} %gather_fusion.1) | data formatting | bytes 393216 | tf_op jit(solution)/shard_map/jit(_take)/gather | solution.py:120
  148.7 4.4 %slice_reduce_fusion.1 = (f32[64]{0:T(128)S(1)}, f32[64]{0:T(128)S(1)}, f32[64]{0:T(128)S(1)}, f32[64]{0:T(128)S(1)}, f32[64]{0:T(128)S(1)}, /*index=5*/f32[64]{...) fusion(f32[6,6,64]{0,1,2:T(8,128)S(1)} %convolution_bitcast_fusion), kind=kLoop, calls=%fused_computation.36 | loop fusion | bytes 9728 | tf_op jit(solution)/shard_map/slice | solution.py:64
  153.1 1.1 slice_reduce_fusion.19
  157.0 2.7 %copy.229 = f32[6,8192]{0,1:T(8,128)} copy(f32[6,8192]{1,0:T(8,128)S(1)} %stack.4) | data formatting | bytes 393216 | tf_op jit(solution)/shard_map/stack | solution.py:51
  159.7 9.7 %gather_fusion.2 = f32[4608,6]{1,0:T(8,128)S(1)} fusion(f32[6,8192]{0,1:T(8,128)} %copy.229, s32[5120]{0:T(1024)S(1)} %pad_clamp_fusion.1), kind=kCustom, calls=%fused_computation.2 | custom fusion | bytes 239616 | tf_op jit(solution)/shard_map/jit(_take)/gather | solution.py:125
  170.9 1.2 reshape.2626
  172.1 9.0 %all-to-all-start.2 = ((f32[32,1,864]{2,1,0:T(1,128)}), f32[32,1,864]{2,1,0:T(1,128)S(1)}, u32[]{:S(2)}, u32[]{:S(2)}) async-start(f32[32,1,864]{2,1,0:T(1,128)} %reshape.2626), calls=%async_computation.2 | async-start | bytes 229376 | tf_op jit(solution)/shard_map/all_to_all | solution.py:128
  181.3 7.4 %all-to-all-done.2 = f32[32,1,864]{2,1,0:T(1,128)S(1)} async-done(((f32[32,1,864]{2,1,0:T(1,128)}), f32[32,1,864]{2,1,0:T(1,128)S(1)}, u32[]{:S(2)}, u32[]{:S(2)}) %all-to-all-start.2) | async-done | bytes 110624 | tf_op jit(solution)/shard_map/all_to_all | solution.py:128
  191.3 3.4 %all-to-all-start.3 = ((f32[8,1,3456]{2,1,0:T(1,128)}), f32[8,1,3456]{2,1,0:T(1,128)S(1)}, u32[]{:S(2)}, u32[]{:S(2)}) async-start(f32[8,1,3456]{2,1,0:T(1,128)} %reshape.2628), calls=%async_computation.3 | async-start | bytes 221184 | tf_op jit(solution)/shard_map/all_to_all | solution.py:127
  194.7 5.1 %stack.5 = f32[36,64]{1,0:T(8,128)} concatenate(f32[1,64]{1,0:T(1,128)S(1)} %bitcast.233, f32[1,64]{1,0:T(1,128)S(1)} %get-tuple-element.133, f32[1,64]{1,0:T(1,128)S(1)} %get-tuple-element.134, f32[1,64]{1,0:T(1,128)S(1)} %get-tuple-element.135, f32[1,64]{1,0:T(1,128)S(1)} %get-tuple-element.138, f32[1,64]{1,0:T(1,128)S(1)} %get-tuple-element.137, f32[1,64]{1,0:T(1,128)S(1)} %broadcast.351, ...), dimensions={0} | concatenate | bytes 18432 | tf_op jit(solution)/shard_map/stack | solution.py:71
  199.8 2.6 %all-to-all-done.3 = f32[8,1,3456]{2,1,0:T(1,128)S(1)} async-done(((f32[8,1,3456]{2,1,0:T(1,128)}), f32[8,1,3456]{2,1,0:T(1,128)S(1)}, u32[]{:S(2)}, u32[]{:S(2)}) %all-to-all-start.3) | async-done | bytes 110624 | tf_op jit(solution)/shard_map/all_to_all | solution.py:127
  204.5 4.5 %copy.234 = f32[6,12801]{0,1:T(8,128)} copy(f32[6,12801]{1,0:T(8,128)S(1)} %concatenate.8) | data formatting | bytes 614448 | tf_op jit(solution)/shard_map/concatenate | solution.py:138
  209.1 12.2 %gather_fusion.3 = f32[4608,6]{1,0:T(8,128)} fusion(f32[6,12801]{0,1:T(8,128)} %copy.234, s32[5120]{0:T(1024)S(1)} %pad_clamp_fusion), kind=kCustom, calls=%fused_computation.3 | custom fusion | bytes 239616 | tf_op jit(solution)/shard_map/jit(_take)/gather | solution.py:138
  221.2 3.8 %select_bitcast_fusion = f32[6,4608]{0,1:T(8,128)S(1)} fusion(f32[4608,6]{1,0:T(8,128)} %gather_fusion.3, pred[4608]{0:T(1024)(128)(4,1)S(1)} %compare_and_fusion.3), kind=kLoop, calls=%fused_computation.8 | loop fusion | flops 27648 | bytes 225792 | tf_op jit(solution)/shard_map/jit(_take)/select_n | solution.py:138
  225.1 1.4 copy.235
  (93 shorter events, 16.4 us)
Async XLA Ops:
  15.1 12.7 %copy-start.4 = (s32[1,256,18]{1,0,2:T(1,128)S(1)}, s32[1,256,18]{1,0,2:T(1,128)}, u32[]{:S(2)}) copy-start(s32[1,256,18]{1,0,2:T(1,128)} %param.11) | copy-start | bytes 55300
  15.1 13.2 %copy-start.1 = (s32[4608]{0:T(1024)S(1)}, s32[4608]{0:T(1024)}, u32[]{:S(2)}) copy-start(s32[4608]{0:T(1024)} %param.9) | copy-start | bytes 55300
  15.1 13.2 %copy-start.2 = (s32[4608]{0:T(1024)S(1)}, s32[4608]{0:T(1024)}, u32[]{:S(2)}) copy-start(s32[4608]{0:T(1024)} %param.8) | copy-start | bytes 55300
  15.1 13.2 %copy-start.3 = (s32[4608]{0:T(1024)S(1)}, s32[4608]{0:T(1024)}, u32[]{:S(2)}) copy-start(s32[4608]{0:T(1024)} %param.7) | copy-start | bytes 55300
  19.2 61.6 %all-to-all-start = ((f32[32,1,864]{2,1,0:T(1,128)}), f32[32,1,864]{2,1,0:T(1,128)S(1)}, u32[]{:S(2)}, u32[]{:S(2)}) async-start(f32[32,1,864]{2,1,0:T(1,128)} %reshape.2622), calls=%async_computation | async-start | bytes 229376 | tf_op jit(solution)/shard_map/all_to_all | solution.py:101
  85.9 15.8 %all-to-all-start.1 = ((f32[8,1,3456]{2,1,0:T(1,128)}), f32[8,1,3456]{2,1,0:T(1,128)S(1)}, u32[]{:S(2)}, u32[]{:S(2)}) async-start(f32[8,1,3456]{2,1,0:T(1,128)} %reshape.2624), calls=%async_computation.1 | async-start | bytes 221184 | tf_op jit(solution)/shard_map/all_to_all | solution.py:100
  157.0 47.4 %copy-start = (f32[6,8192]{1,0:T(8,128)}, f32[6,8192]{1,0:T(8,128)S(1)}, u32[]{:S(2)}) copy-start(f32[6,8192]{1,0:T(8,128)S(1)} %stack.4) | copy-start | bytes 589828
  172.1 16.5 %all-to-all-start.2 = ((f32[32,1,864]{2,1,0:T(1,128)}), f32[32,1,864]{2,1,0:T(1,128)S(1)}, u32[]{:S(2)}, u32[]{:S(2)}) async-start(f32[32,1,864]{2,1,0:T(1,128)} %reshape.2626), calls=%async_computation.2 | async-start | bytes 229376 | tf_op jit(solution)/shard_map/all_to_all | solution.py:128
  191.3 11.1 %all-to-all-start.3 = ((f32[8,1,3456]{2,1,0:T(1,128)}), f32[8,1,3456]{2,1,0:T(1,128)S(1)}, u32[]{:S(2)}, u32[]{:S(2)}) async-start(f32[8,1,3456]{2,1,0:T(1,128)} %reshape.2628), calls=%async_computation.3 | async-start | bytes 221184 | tf_op jit(solution)/shard_map/all_to_all | solution.py:127
where the time goes:
time: 227 us; the launch traced here: 226 us
  local copies, waits for them, and re-layouts  161 us (71%)
  starting transfers between devices  29.2 us (13%)
  waiting for transfers between devices  17.6 us (8%)
  other arithmetic  17.2 us (8%)
    gather x2, local copies, waits for them, and re-layouts, body(): jnp.take(jnp.concatenate([nullspace, arrived, zero_column], axis=1), slot...  33.1 us
    scatter x1, local copies, waits for them, and re-layouts, body(): slot_source.at[landing_safe].set(row_count + arrive_ids, mode='drop')  17.5 us
    scatter x1, local copies, waits for them, and re-layouts, body(): fine_source.at[jnp.where(live_out, outgoing, row_count)]  17.4 us
    scatter x1, local copies, waits for them, and re-layouts, body(): slot_source = slot_source.at[local_slot].set(row_ids, mode='drop')  17.4 us
    gather x3, local copies, waits for them, and re-layouts, body(): picked = jnp.take(nullspace, jnp.where(live_out, outgoing, 0), axis=1)  12.5 us
    unnamed x22, local copies, waits for them, and re-layouts  12.3 us
    gather x1, local copies, waits for them, and re-layouts, body(): jnp.take(jnp.concatenate([padded_q, zero_column, returned], axis=1), fine...  12.2 us
    gather x3, local copies, waits for them, and re-layouts, body(): answer = jnp.take(padded_q, jnp.where(live_in, landing, 0), axis=1)  11.2 us
  transfers between devices with their start and end apart: 4, of which 3 were waited for; matrix products, arithmetic and copies ran while one was open for 26% of the time, Pallas kernels for 0%

commit v1 on v0

v1 whole, which is shorter than its diff:
```python
import jax
import jax.numpy as jnp
from jax import lax
from jax.experimental import pallas as pl
from jax.experimental.pallas import tpu as pltpu
from jax.sharding import PartitionSpec as P

PAD = 128
AGG_DEV = 64
MODES = 6
ROWS = 4608
CHUNKS = 36
LANES = 18
PEERS = 256
GROUPS = (0, 8, 16, 24, 28)
AXES = ("dom", "slab")


def lane_take(table_row, lane_index):
    wide = jnp.broadcast_to(table_row, lane_index.shape)
    return jnp.take_along_axis(wide, lane_index, axis=1, mode="promise_in_bounds")


def row_iota(shape, dtype=jnp.int32):
    return lax.broadcasted_iota(jnp.int32, shape, 0).astype(dtype)


def one_hot_rows(values_row, iota_rows, scaled=None):
    hit = iota_rows == values_row
    payload = jnp.ones_like(iota_rows) if scaled is None else scaled
    return jnp.where(hit, payload, jnp.zeros_like(iota_rows))


def nt_dot(left, right):
    return lax.dot_general(left, right, (((1,), (1,)), ((), ())), preferred_element_type=jnp.float32)


def pick_kernel(rows_ref, sent_ref, send_ref, gathered_ref, message_ref):
    index = [jnp.maximum(sent_ref[g : g + 8, :], 0) for g in GROUPS]
    lane = [v & 127 for v in index]
    tile = [v >> 7 for v in index]
    for half in (slice(0, 3), slice(3, 6)):
        modes = range(MODES)[half]
        acc = {(m, g): jnp.zeros((8, 128), jnp.float32) for m in modes for g in range(5)}
        for t in range(CHUNKS):
            hits = [v == t for v in tile]
            for m in modes:
                row = rows_ref[m : m + 1, t * 128 : (t + 1) * 128]
                for g in range(5):
                    acc[m, g] = jnp.where(hits[g], lane_take(row, lane[g]), acc[m, g])
        for m in modes:
            for g in range(5):
                gathered_ref[m, GROUPS[g] : GROUPS[g] + 8, :] = acc[m, g]
    for h in range(2):
        message_ref[...] = jnp.zeros((128, 128), jnp.float32)
        for m in range(MODES):
            message_ref[pl.ds(m, LANES, stride=MODES), :] = gathered_ref[m, pl.ds(h, LANES, stride=2), :]
        send_ref[h * 128 : (h + 1) * 128, :] = message_ref[...].T


def split3(value):
    top = value.astype(jnp.bfloat16)
    rest = value - top.astype(jnp.float32)
    mid = rest.astype(jnp.bfloat16)
    low = (rest - mid.astype(jnp.float32)).astype(jnp.bfloat16)
    return top, mid, low


def gram_part(rows_of, aggregate_ref, left_ref, right_ref):
    agg_iota = row_iota((AGG_DEV, 128), jnp.bfloat16)
    for c in range(CHUNKS):
        cols = slice(c * 128, (c + 1) * 128)
        x = rows_of(c)
        for i in range(0, MODES, 2):
            pieces = split3(jnp.concatenate([x * x[i : i + 1, :], x * x[i + 1 : i + 2, :]], axis=0))
            for s in range(3):
                left_ref[s * 48 + i * 8 : s * 48 + i * 8 + 16, cols] = pieces[s]
        agg = aggregate_ref[c : c + 1, :].astype(jnp.float32).astype(jnp.bfloat16)
        right_ref[:, cols] = one_hot_rows(agg, agg_iota)
    full = nt_dot(left_ref[...], right_ref[...])
    return full[0:48] + (full[48:96] + full[96:144])


def own_kernel(me_ref, rows_ref, owner_ref, local_ref, place_ref, sent_ref, arrive_ref,
               gram_ref, fine_source_ref, slot_source_ref,
               rows8_ref, agg_ref, left_ref, right_ref, fl_ref, fr_ref, sl_ref, sr_ref):
    me = me_ref[0]
    owned = owner_ref[...] == me
    agg_ref[...] = jnp.where(owned, local_ref[...], -1)
    rows8_ref[0:MODES, :] = rows_ref[...]
    rows8_ref[MODES:8, :] = jnp.zeros((2, ROWS), jnp.float32)
    gram_ref[...] = gram_part(lambda c: rows8_ref[:, c * 128 : (c + 1) * 128], agg_ref, left_ref, right_ref)
    lane_row = lax.broadcasted_iota(jnp.int32, (1, 128), 1).astype(jnp.float32).astype(jnp.bfloat16)
    low_iota = row_iota((128, 128)).astype(jnp.float32).astype(jnp.bfloat16)
    hi48 = row_iota((48, 128)).astype(jnp.float32).astype(jnp.bfloat16)
    hi64 = row_iota((64, 128)).astype(jnp.float32).astype(jnp.bfloat16)
    lanes48 = jnp.broadcast_to(lane_row, (48, 128))
    lanes64 = jnp.broadcast_to(lane_row, (64, 128))

    def as_row(value):
        return value.astype(jnp.float32).astype(jnp.bfloat16)

    def part(c, hi_row, lo_row, hi_iota, lanes, left, right, number):
        cols = slice(c * 128, (c + 1) * 128)
        count = hi_iota.shape[0]
        left[0:count, cols] = one_hot_rows(hi_row, hi_iota, jnp.full_like(hi_iota, number))
        left[count : 2 * count, cols] = one_hot_rows(hi_row, hi_iota, lanes)
        right[:, cols] = one_hot_rows(lo_row, low_iota)

    for c in range(CHUNKS):
        sent = sent_ref[c : c + 1, :]
        part(c, as_row(sent >> 7), as_row(sent & 127), hi48, lanes48, fl_ref, fr_ref, c)
        part(c, as_row(agg_ref[c : c + 1, :]), as_row(place_ref[c : c + 1, :]), hi64, lanes64, sl_ref, sr_ref, c + 1)
        landing = arrive_ref[c : c + 1, :]
        part(CHUNKS + c, as_row(landing >> 7), as_row(landing & 127), hi64, lanes64, sl_ref, sr_ref, CHUNKS + c + 1)
    found = nt_dot(fl_ref[...], fr_ref[...])
    code = (found[0:48] * 128.0 + found[48:96]).astype(jnp.int32)
    fine_source_ref[...] = jnp.where(owned, -1, code[0:CHUNKS])
    found = nt_dot(sl_ref[...], sr_ref[...])
    slot_source_ref[...] = (found[0:64] * 128.0 + found[64:128]).astype(jnp.int32) - 128


def apply_tables(x, agg_row, table_ref):
    index = jnp.broadcast_to(agg_row, (8, 128))
    total = None
    for i in range(MODES):
        entry = jnp.take_along_axis(table_ref[i * 8 : (i + 1) * 8, :], index, axis=1, mode="promise_in_bounds")
        term = jnp.broadcast_to(x[i : i + 1, :], (8, 128)) * entry
        total = term if total is None else total + term
    return total


def factor_kernel(recv_ref, arrive_ref, gram_ref, send_ref, coarse_ref, table_ref, answer_ref,
                  rows8_ref, agg_ref, left_ref, right_ref, message_ref):
    landing = arrive_ref[...]
    agg_ref[...] = jnp.where(landing >= 0, landing >> 7, -1)
    rows8_ref[MODES:8, :] = jnp.zeros((2, ROWS), jnp.float32)
    for h in range(2):
        message_ref[...] = recv_ref[h * 128 : (h + 1) * 128, :].T
        for k in range(LANES):
            c = 2 * k + h
            rows8_ref[0:MODES, c * 128 : (c + 1) * 128] = message_ref[MODES * k : MODES * (k + 1), :]
    gram = gram_ref[...] + gram_part(lambda c: rows8_ref[:, c * 128 : (c + 1) * 128], agg_ref, left_ref, right_ref)
    g = [[gram[i * 8 + j : i * 8 + j + 1, :] for j in range(MODES)] for i in range(MODES)]
    up = [[None] * MODES for _ in range(MODES)]
    over = [None] * MODES
    zero = jnp.zeros((1, AGG_DEV), jnp.float32)
    for i in range(MODES):
        square = g[i][i]
        for k in range(i):
            square = square - up[k][i] * up[k][i]
        pivot = jnp.sqrt(square)
        up[i][i] = pivot
        over[i] = 1.0 / pivot
        for j in range(i + 1, MODES):
            rest = g[i][j]
            for k in range(i):
                rest = rest - up[k][i] * up[k][j]
            up[i][j] = rest * over[i]
    inv = [[None] * MODES for _ in range(MODES)]
    for i in range(MODES):
        inv[i][i] = over[i]
        for j in range(i + 1, MODES):
            total = inv[i][i] * up[i][j]
            for k in range(i + 1, j):
                total = total + inv[i][k] * up[k][j]
            inv[i][j] = -total * over[j]
    table_ref[...] = jnp.zeros((48, 128), jnp.float32)
    for i in range(MODES):
        for j in range(MODES):
            coarse_ref[i * MODES + j : i * MODES + j + 1, :] = up[i][j] if j >= i else zero
            if j >= i:
                table_ref[i * 8 + j : i * 8 + j + 1, 0:AGG_DEV] = inv[i][j]
    for h in range(2):
        message_ref[...] = jnp.zeros((128, 128), jnp.float32)
        for k in range(LANES):
            c = 2 * k + h
            cols = slice(c * 128, (c + 1) * 128)
            index = jnp.maximum(agg_ref[c : c + 1, :], 0)
            answer = apply_tables(rows8_ref[:, cols], index, table_ref)
            answer_ref[:, cols] = answer
            message_ref[MODES * k : MODES * (k + 1), :] = answer[0:MODES]
        send_ref[h * 128 : (h + 1) * 128, :] = message_ref[...].T


def padded_kernel(rows_ref, local_ref, table_ref, answer_ref, source_ref, padded_ref, own_ref, placed_ref):
    for c in range(CHUNKS):
        cols = slice(c * 128, (c + 1) * 128)
        own_ref[:, cols] = apply_tables(rows_ref[:, cols], local_ref[c : c + 1, :], table_ref)
    code = [source_ref[g * 8 : (g + 1) * 8, :] for g in range(8)]
    lane = [v & 127 for v in code]
    tile = [v >> 7 for v in code]
    for half in range(3):
        modes = range(2 * half, 2 * half + 2)
        acc = {(m, g): jnp.zeros((8, 128), jnp.float32) for m in modes for g in range(8)}
        for t in range(2 * CHUNKS):
            hits = [v == t for v in tile]
            part = own_ref if t < CHUNKS else answer_ref
            at = (t % CHUNKS) * 128
            for m in modes:
                row = part[m : m + 1, at : at + 128]
                for g in range(8):
                    acc[m, g] = jnp.where(hits[g], lane_take(row, lane[g]), acc[m, g])
        for m in modes:
            for g in range(8):
                placed_ref[m * 64 + g * 8 : m * 64 + g * 8 + 8, :] = acc[m, g]
    for a in range(AGG_DEV):
        padded_ref[:, a * 128 : (a + 1) * 128] = placed_ref[pl.ds(a, MODES, stride=AGG_DEV), :]


def fine_kernel(recv_ref, source_ref, own_ref, fine_ref, message_ref, placed_ref):
    for h in range(2):
        message_ref[h * 128 : (h + 1) * 128, :] = recv_ref[h * 128 : (h + 1) * 128, :].T
    code = [source_ref[g : g + 8, :] for g in GROUPS]
    lane = [v & 127 for v in code]
    tile = [v >> 7 for v in code]
    for half in (slice(0, 3), slice(3, 6)):
        modes = range(MODES)[half]
        acc = {(m, g): jnp.zeros((8, 128), jnp.float32) for m in modes for g in range(5)}
        for t in range(CHUNKS):
            hits = [v == t for v in tile]
            for m in modes:
                at = (t % 2) * 128 + MODES * (t // 2) + m
                row = message_ref[at : at + 1, :]
                for g in range(5):
                    acc[m, g] = jnp.where(hits[g], lane_take(row, lane[g]), acc[m, g])
        for m in modes:
            for g in range(5):
                placed_ref[m * 40 + GROUPS[g] : m * 40 + GROUPS[g] + 8, :] = acc[m, g]
    for c in range(CHUNKS):
        cols = slice(c * 128, (c + 1) * 128)
        away = jnp.broadcast_to(source_ref[c : c + 1, :] >= 0, (MODES, 128))
        fine_ref[:, cols] = jnp.where(away, placed_ref[pl.ds(c, MODES, stride=40), :], own_ref[0:MODES, cols])


def f32(*shape):
    return jax.ShapeDtypeStruct(shape, jnp.float32)


def i32(*shape):
    return jax.ShapeDtypeStruct(shape, jnp.int32)


def vm(*shape):
    return pltpu.VMEM(shape, jnp.float32)


def vb(*shape):
    return pltpu.VMEM(shape, jnp.bfloat16)


def call(kernel, out_shape, scratch, *args, scalar=False):
    specs = [pl.BlockSpec(memory_space=pltpu.VMEM) for _ in args]
    if scalar:
        specs[0] = pl.BlockSpec(memory_space=pltpu.SMEM)
    many = isinstance(out_shape, tuple)
    one = pl.BlockSpec(memory_space=pltpu.VMEM)
    return pl.pallas_call(
        kernel,
        out_shape=out_shape,
        in_specs=specs,
        out_specs=tuple(one for _ in out_shape) if many else one,
        scratch_shapes=scratch,
        compiler_params=pltpu.CompilerParams(vmem_limit_bytes=40 * 1024 * 1024),
        name=kernel.__name__,
    )(*args)


def exchange(message):
    return lax.all_to_all(message, AXES, 0, 0, tiled=True)


def body(nullspace, owner_device, local_aggregate, position, sent_rows, arrival_slot):
    me = (lax.axis_index("dom") * lax.axis_size("slab") + lax.axis_index("slab")).reshape(1)
    owner = owner_device.reshape(CHUNKS, 128)
    local = local_aggregate.reshape(CHUNKS, 128)
    place = position.reshape(CHUNKS, 128)
    sent = jnp.transpose(sent_rows[0], (1, 0)).reshape(CHUNKS, 128)
    arrive = jnp.transpose(arrival_slot[0], (1, 0)).reshape(CHUNKS, 128)
    send = call(pick_kernel, f32(PEERS, 128), [vm(MODES, 40, 128), vm(128, 128)], nullspace, sent)
    recv = exchange(send)
    gram_scratch = [vm(8, ROWS), pltpu.VMEM((CHUNKS, 128), jnp.int32), vb(144, ROWS), vb(AGG_DEV, ROWS)]
    gram, fine_source, slot_source = call(
        own_kernel,
        (f32(48, AGG_DEV), i32(CHUNKS, 128), i32(AGG_DEV, 128)),
        gram_scratch + [vb(96, ROWS), vb(128, ROWS), vb(128, 2 * ROWS), vb(128, 2 * ROWS)],
        me, nullspace, owner, local, place, sent, arrive,
        scalar=True,
    )
    send, coarse, table, answer = call(
        factor_kernel,
        (f32(PEERS, 128), f32(36, AGG_DEV), f32(48, 128), f32(8, ROWS)),
        gram_scratch + [vm(128, 128)],
        recv, arrive, gram,
    )
    recv = exchange(send)
    padded, own = call(
        padded_kernel,
        (f32(MODES, AGG_DEV * PAD), f32(8, ROWS)),
        [vm(MODES * AGG_DEV, 128)],
        nullspace, local, table, answer, slot_source,
    )
    fine = call(
        fine_kernel,
        f32(MODES, ROWS),
        [vm(256, 128), vm(MODES * 40, 128)],
        recv, fine_source, own,
    )
    return fine, padded, coarse


def solution(mesh):
    in_specs = (
        P(None, AXES),
        P(AXES),
        P(AXES),
        P(AXES),
        P(AXES, None, None),
        P(AXES, None, None),
    )
    out_specs = (P(None, AXES), P(None, AXES), P(None, AXES))
    return jax.shard_map(body, mesh=mesh, in_specs=in_specs, out_specs=out_specs, check_vma=False)
```

time: 227 us -> 59.8 us (0.26)
  local copies, waits for them, and re-layouts: 161 us -> 2.36 us
  Pallas kernels: 0 us -> 23.4 us
  other arithmetic: 17.2 us -> 0 us
  starting transfers between devices: 29.2 us -> 21.2 us
  waiting for transfers between devices: 17.6 us -> 11.7 us
    gather x9 -> x0, local copies, waits for them, and re-layouts: 69 us -> none  [the longest x2 33.1 us: body(): jnp.take(jnp.concatenate([nullspace, arrived, zero_column], axis=1), slot...]
    scatter x3 -> x0, local copies, waits for them, and re-layouts: 52.3 us -> none  [the longest x1 17.5 us: body(): slot_source.at[landing_safe].set(row_count + arrive_ids, mode='drop')]
    pallas_call x0 -> x5, Pallas kernels: none -> 23.4 us  [call(): pl.pallas_call(kernel, out_shape=out_shape, in_specs=specs, out_specs=tup...]
    unnamed x22 -> x14, local copies, waits for them, and re-layouts: 12.3 us -> 2.35 us
    another operation x7 -> x0, local copies, waits for them, and re-layouts: 8.06 us -> none  [the longest x1 5.09 us: factor_block(): jnp.stack([factor_up[left_i][right_j] for left_i in range(mode_count) for...]
    all_to_all x4 -> x2, starting transfers between devices: 29.2 us -> 21.2 us  [exchange(): return lax.all_to_all(message, AXES, 0, 0, tiled=True)]
    concatenate x1 -> x0, other arithmetic: 7.29 us -> none  [body(): jnp.concatenate([nullspace, arrived, zero_column], axis=1)]
    all_to_all x4 -> x2, waiting for transfers between devices: 17.6 us -> 11.7 us  [exchange(): return lax.all_to_all(message, AXES, 0, 0, tiled=True)]
  transfers between devices with their start and end apart: 4 -> 2, of which waited for: 3 -> 2; matrix products, arithmetic and copies ran while one was open for 26% -> 0% of each run, Pallas kernels for 0% -> 23%
where the time goes in v1:
time: 59.8 us; the launch traced here: 59.5 us
  Pallas kernels  23.4 us (39%)
  starting transfers between devices  21.2 us (35%)
  waiting for transfers between devices  11.7 us (20%)
  local copies, waits for them, and re-layouts  2.36 us (4%)
  between operations  0.73 us (1%)
    pallas_call x5, Pallas kernels, call(): pl.pallas_call(kernel, out_shape=out_shape, in_specs=specs, out_specs=tup...  23.4 us
    all_to_all x2, starting transfers between devices, exchange(): return lax.all_to_all(message, AXES, 0, 0, tiled=True)  21.2 us
    all_to_all x2, waiting for transfers between devices, exchange(): return lax.all_to_all(message, AXES, 0, 0, tiled=True)  11.7 us
    unnamed x14, local copies, waits for them, and re-layouts  2.35 us
  transfers between devices with their start and end apart: 2, of which 2 were waited for; matrix products, arithmetic and copies ran while one was open for 0% of the time, Pallas kernels for 23%

profile of v1, /device:TPU:1, one launch (start us, length us, event | category | flops | bytes accessed | tf_op | source)
XLA Modules:
  0.0 59.5 jit_solution(7769122167611558113)
XLA Ops:
  0.6 0.7 %copy.16 = s32[1,256,18]{1,2,0:T(8,128)S(1)} copy(s32[1,256,18]{1,0,2:T(1,128)} %param.10) | data formatting | bytes 36864
  1.4 0.0 copy-start
  1.4 0.9 %copy-done = f32[6,4608]{1,0:T(8,128)S(1)} copy-done((f32[6,4608]{1,0:T(8,128)S(1)}, f32[6,4608]{1,0:T(8,128)}, u32[]{:S(2)}) %copy-start) | copy-done | bytes 110616
  2.3 3.9 %pick_kernel.1 = f32[256,128]{1,0:T(8,128)} custom-call(f32[6,4608]{1,0:T(8,128)S(1)} %copy-done, s32[36,128]{1,0:T(8,128)S(1)} %reshape.28.sent_ref), custom_call_target="tpu_custom_call" | custom-call | tf_op jit(solution)/shard_map/pick_kernel/pallas_call | solution.py:258
  6.2 0.0 copy-start.5
  6.2 0.0 copy-start.1
  6.2 15.7 %all-to-all-start = ((f32[256,1,128]{2,1,0:T(1,128)}), f32[256,1,128]{2,1,0:T(1,128)S(1)}, u32[]{:S(2)}, u32[]{:S(2)}) async-start(f32[256,1,128]{2,1,0:T(1,128)} %bitcast.2), calls=%async_computation | async-start | bytes 262144 | tf_op jit(solution)/shard_map/all_to_all | solution.py:270
  21.8 0.0 copy-done.5
  21.8 0.0 copy-start.4
  21.9 0.0 copy-start.2
  21.9 0.0 copy-start.3
  21.9 0.0 copy-done.1
  21.9 0.7 %copy-done.4 = s32[4608]{0:T(1024)S(1)} copy-done((s32[4608]{0:T(1024)S(1)}, s32[4608]{0:T(1024)}, u32[]{:S(2)}) %copy-start.4) | copy-done | bytes 18456
  22.6 0.0 copy-done.2
  22.6 0.0 copy-done.3
  22.6 2.4 %own_kernel.1 = (f32[48,64]{1,0:T(8,128)S(1)}, s32[36,128]{1,0:T(8,128)S(1)}, s32[64,128]{1,0:T(8,128)S(1)}) custom-call(s32[1]{0:T(128)} %bitcast.5.me_ref, f32[6,4608]{1,0:T(8,128)S(1)} %copy-done.1, s32[36,128]{1,0:T(8,128)S(1)} %bitcast.26, s32[36,128]{1,0:T(8,128)S(1)} %bitcast.24, s32[36,128]{1,0:T(8,128)S(1)} %bitcast.27, ...), custom_call_target="tpu_custom_call" | custom-call | tf_op jit(solution)/shard_map/own_kernel/pallas_call | solution.py:258
  25.0 9.8 %all-to-all-done = f32[256,1,128]{2,1,0:T(1,128)S(1)} async-done(((f32[256,1,128]{2,1,0:T(1,128)}), f32[256,1,128]{2,1,0:T(1,128)S(1)}, u32[]{:S(2)}, u32[]{:S(2)}) %all-to-all-start) | async-done | bytes 131104 | tf_op jit(solution)/shard_map/all_to_all | solution.py:270
  34.8 2.1 %factor_kernel.1 = (f32[256,128]{1,0:T(8,128)}, f32[36,64]{1,0:T(8,128)}, f32[48,128]{1,0:T(8,128)S(1)}, f32[8,4608]{1,0:T(8,128)S(1)}) custom-call(f32[256,128]{1,0:T(8,128)S(1)} %bitcast.23, s32[36,128]{1,0:T(8,128)S(1)} %reshape.29.arrive_ref, f32[48,64]{1,0:T(8,128)S(1)} %get-tuple-element.12.gram_ref), custom_call_target="tpu_custom_call" | custom-call | tf_op jit(solution)/shard_map/factor_kernel/pallas_call | solution.py:258
  36.9 5.6 %all-to-all-start.1 = ((f32[256,1,128]{2,1,0:T(1,128)}), f32[256,1,128]{2,1,0:T(1,128)S(1)}, u32[]{:S(2)}, u32[]{:S(2)}) async-start(f32[256,1,128]{2,1,0:T(1,128)} %bitcast.10), calls=%async_computation.1 | async-start | bytes 262144 | tf_op jit(solution)/shard_map/all_to_all | solution.py:270
  42.4 11.1 %padded_kernel.1 = (f32[6,8192]{1,0:T(8,128)}, f32[8,4608]{1,0:T(8,128)S(1)}) custom-call(f32[6,4608]{1,0:T(8,128)S(1)} %copy-done.1, s32[36,128]{1,0:T(8,128)S(1)} %bitcast.25, f32[48,128]{1,0:T(8,128)S(1)} %get-tuple-element.15.table_ref, f32[8,4608]{1,0:T(8,128)S(1)} %get-tuple-element.16.answer_ref, s32[64,128]{1,0:T(8,128)S(1)} %get-tuple-element.17.source_ref), custom_call_target="tpu_custom_call" | custom-call | tf_op jit(solution)/shard_map/padded_kernel/pallas_call | solution.py:258
  53.6 1.9 %all-to-all-done.1 = f32[256,1,128]{2,1,0:T(1,128)S(1)} async-done(((f32[256,1,128]{2,1,0:T(1,128)}), f32[256,1,128]{2,1,0:T(1,128)S(1)}, u32[]{:S(2)}, u32[]{:S(2)}) %all-to-all-start.1) | async-done | bytes 131104 | tf_op jit(solution)/shard_map/all_to_all | solution.py:270
  55.5 3.9 %fine_kernel.1 = f32[6,4608]{1,0:T(8,128)} custom-call(f32[256,128]{1,0:T(8,128)S(1)} %bitcast.22, s32[36,128]{1,0:T(8,128)S(1)} %get-tuple-element.14.source_ref, f32[8,4608]{1,0:T(8,128)S(1)} %get-tuple-element.18.own_ref), custom_call_target="tpu_custom_call" | custom-call | tf_op jit(solution)/shard_map/fine_kernel/pallas_call | solution.py:258
  (3 shorter events, 0.0 us)
Async XLA Ops:
  1.4 0.9 %copy-start = (f32[6,4608]{1,0:T(8,128)S(1)}, f32[6,4608]{1,0:T(8,128)}, u32[]{:S(2)}) copy-start(f32[6,4608]{1,0:T(8,128)} %rows_ref.5) | copy-start | bytes 331780
  6.2 15.7 %copy-start.5 = (s32[1,256,18]{1,0,2:T(1,128)S(1)}, s32[1,256,18]{1,0,2:T(1,128)}, u32[]{:S(2)}) copy-start(s32[1,256,18]{1,0,2:T(1,128)} %param.11) | copy-start | bytes 55300
  6.2 15.8 %copy-start.1 = (f32[6,4608]{1,0:T(8,128)S(1)}, f32[6,4608]{1,0:T(8,128)}, u32[]{:S(2)}) copy-start(f32[6,4608]{1,0:T(8,128)} %rows_ref.5) | copy-start | bytes 331780
  6.2 28.6 %all-to-all-start = ((f32[256,1,128]{2,1,0:T(1,128)}), f32[256,1,128]{2,1,0:T(1,128)S(1)}, u32[]{:S(2)}, u32[]{:S(2)}) async-start(f32[256,1,128]{2,1,0:T(1,128)} %bitcast.2), calls=%async_computation | async-start | bytes 262144 | tf_op jit(solution)/shard_map/all_to_all | solution.py:270
  21.8 0.7 %copy-start.4 = (s32[4608]{0:T(1024)S(1)}, s32[4608]{0:T(1024)}, u32[]{:S(2)}) copy-start(s32[4608]{0:T(1024)} %param.9) | copy-start | bytes 55300
  21.9 0.7 %copy-start.2 = (s32[4608]{0:T(1024)S(1)}, s32[4608]{0:T(1024)}, u32[]{:S(2)}) copy-start(s32[4608]{0:T(1024)} %param.8) | copy-start | bytes 55300
  21.9 0.7 %copy-start.3 = (s32[4608]{0:T(1024)S(1)}, s32[4608]{0:T(1024)}, u32[]{:S(2)}) copy-start(s32[4608]{0:T(1024)} %param.7) | copy-start | bytes 55300
  36.9 18.7 %all-to-all-start.1 = ((f32[256,1,128]{2,1,0:T(1,128)}), f32[256,1,128]{2,1,0:T(1,128)S(1)}, u32[]{:S(2)}, u32[]{:S(2)}) async-start(f32[256,1,128]{2,1,0:T(1,128)} %bitcast.10), calls=%async_computation.1 | async-start | bytes 262144 | tf_op jit(solution)/shard_map/all_to_all | solution.py:270

commit v2 on v1

v2 whole, which is shorter than its diff:
```python
import jax
import jax.numpy as jnp
from jax import lax
from jax.experimental import pallas as pl
from jax.experimental.pallas import tpu as pltpu
from jax.sharding import PartitionSpec as P

PAD = 128
AGG_DEV = 64
MODES = 6
ROWS = 4608
CHUNKS = 36
LANES = 18
PEERS = 256
AXES = ("dom", "slab")


def row_iota(shape, dtype=jnp.int32):
    return lax.broadcasted_iota(jnp.int32, shape, 0).astype(dtype)


def one_hot_rows(values_row, iota_rows, scaled=None):
    hit = iota_rows == values_row
    payload = jnp.ones_like(iota_rows) if scaled is None else scaled
    return jnp.where(hit, payload, jnp.zeros_like(iota_rows))


def as_row(value):
    return value.astype(jnp.float32).astype(jnp.bfloat16)


def nt_dot(left, right):
    return lax.dot_general(left, right, (((1,), (1,)), ((), ())), preferred_element_type=jnp.float32)


def split3(value):
    top = value.astype(jnp.bfloat16)
    rest = value - top.astype(jnp.float32)
    mid = rest.astype(jnp.bfloat16)
    low = (rest - mid.astype(jnp.float32)).astype(jnp.bfloat16)
    return top, mid, low


def pick_kernel(rows_hbm, sent_hbm, send_ref, rows_ref, sent_ref, left_ref, message_ref, arrived):
    sent_copy = pltpu.make_async_copy(sent_hbm, sent_ref, arrived.at[0])
    rows_copy = pltpu.make_async_copy(rows_hbm, rows_ref, arrived.at[1])
    sent_copy.start()
    rows_copy.start()
    rows_copy.wait()
    pad = jnp.zeros((2, 128), jnp.float32)
    for hi in range(0, 18, 2):
        for side in range(2):
            t = 2 * hi + side
            first = rows_ref[:, t * 128 : (t + 1) * 128]
            second = rows_ref[:, (t + 2) * 128 : (t + 3) * 128]
            pair = jnp.concatenate([first, pad, second, pad], axis=0)
            for s, piece in enumerate(split3(pair)):
                left_ref[hi * 8 : hi * 8 + 16, s * 256 + side * 128 : s * 256 + side * 128 + 128] = piece
    sent_copy.wait()
    lane_iota = row_iota((256, 128)).astype(jnp.float32).astype(jnp.bfloat16)
    for h in range(2):
        message_ref[...] = jnp.zeros((128, 128), jnp.float32)
        for k0 in range(0, LANES, 2):
            index = [sent_ref[k, :, h * 128 : (h + 1) * 128] for k in range(k0, k0 + 2)]
            hot = jnp.concatenate([one_hot_rows(as_row(v & 255), lane_iota) for v in index], axis=1)
            found = jnp.dot(left_ref[...], jnp.concatenate([hot] * 3, axis=0), preferred_element_type=jnp.float32)
            for n, v in enumerate(index):
                tile = jnp.broadcast_to(v >> 8, (8, 128))
                total = jnp.zeros((8, 128), jnp.float32)
                for t in range(18):
                    total = jnp.where(tile == t, found[t * 8 : t * 8 + 8, n * 128 : (n + 1) * 128], total)
                k = k0 + n
                message_ref[MODES * k : MODES * (k + 1), :] = total[0:MODES]
        send_ref[h * 128 : (h + 1) * 128, :] = message_ref[...].T


def gram_part(rows8_ref, hot_ref, left_ref):
    for c in range(CHUNKS):
        cols = slice(c * 128, (c + 1) * 128)
        x = rows8_ref[:, cols]
        for i in range(0, MODES, 2):
            one = jnp.broadcast_to(rows8_ref[i : i + 1, cols], (8, 128))
            two = jnp.broadcast_to(rows8_ref[i + 1 : i + 2, cols], (8, 128))
            pieces = split3(jnp.concatenate([x * one, x * two], axis=0))
            for s in range(3):
                left_ref[s * 48 + i * 8 : s * 48 + i * 8 + 16, cols] = pieces[s]
    full = nt_dot(left_ref[...], hot_ref[...])
    return full[0:48] + (full[48:96] + full[96:144])


def hot_aggregates(agg_row, c, hot_ref):
    iota = row_iota((AGG_DEV, 128)).astype(jnp.float32).astype(jnp.bfloat16)
    hot_ref[:, c * 128 : (c + 1) * 128] = one_hot_rows(as_row(agg_row), iota)


def of_chunk(table_ref, c):
    return table_ref[c // 2, :, (c % 2) * 128 : (c % 2) * 128 + 128]


def own_kernel(me_ref, rows_ref, owner_ref, local_ref, arrive_ref, sent_ref, gram_ref, agg_ref, hot_ref, landed_ref,
               rows8_ref, left_ref):
    owned = owner_ref[...] == me_ref[0]
    agg_ref[...] = jnp.where(owned, local_ref[...], -1)
    rows8_ref[0:MODES, :] = rows_ref[...]
    rows8_ref[MODES:8, :] = jnp.zeros((2, ROWS), jnp.float32)
    for c in range(CHUNKS):
        hot_aggregates(agg_ref[c : c + 1, :], c, hot_ref)
        hot_aggregates(of_chunk(arrive_ref, c) >> 7, c, landed_ref)
    gram_ref[...] = gram_part(rows8_ref, hot_ref, left_ref)


def apply_tables(rows8_ref, hot_ref, table_ref, put):
    table = jnp.concatenate(split3(table_ref[...]), axis=1)
    step = 2
    for c0 in range(0, CHUNKS, step):
        hot = hot_ref[:, c0 * 128 : (c0 + step) * 128]
        entry = jnp.dot(table, jnp.concatenate([hot] * 3, axis=0), preferred_element_type=jnp.float32)
        for c in range(c0, c0 + step):
            cols = slice(c * 128, (c + 1) * 128)
            part = entry[:, (c - c0) * 128 : (c - c0 + 1) * 128]
            total = jnp.broadcast_to(rows8_ref[0:1, cols], (8, 128)) * part[0:8]
            for i in range(1, MODES):
                total = total + jnp.broadcast_to(rows8_ref[i : i + 1, cols], (8, 128)) * part[i * 8 : i * 8 + 8]
            put(c, total)


def low_part(target_row, c, low_ref):
    iota = row_iota((256, 128)).astype(jnp.float32).astype(jnp.bfloat16)
    low_ref[:, c * 128 : (c + 1) * 128] = one_hot_rows(as_row(target_row & 255), iota)


def high_part(tile, target_row, high_count, c, left_ref):
    top = tile.astype(jnp.bfloat16).astype(jnp.float32)
    pieces = jnp.concatenate([top, tile - top], axis=0).astype(jnp.bfloat16)
    high = jnp.broadcast_to(as_row(target_row >> 8), (16, 128))
    zero = jnp.zeros((16, 128), jnp.bfloat16)
    for hi in range(high_count):
        left_ref[hi * 16 : hi * 16 + 16, c * 128 : (c + 1) * 128] = jnp.where(high == hi, pieces, zero)


def factor_kernel(recv_ref, landed_ref, gram_ref, send_ref, coarse_ref, table_ref, answer_ref,
                  rows8_ref, left_ref, message_ref):
    rows8_ref[MODES:8, :] = jnp.zeros((2, ROWS), jnp.float32)
    for h in range(2):
        message_ref[h] = recv_ref[h * 128 : (h + 1) * 128, :].T
        for k in range(LANES):
            c = 2 * k + h
            rows8_ref[0:MODES, c * 128 : (c + 1) * 128] = message_ref[h, MODES * k : MODES * (k + 1), :]
    gram = gram_ref[...] + gram_part(rows8_ref, landed_ref, left_ref)
    g = [[gram[i * 8 + j : i * 8 + j + 1, :] for j in range(MODES)] for i in range(MODES)]
    up = [[None] * MODES for _ in range(MODES)]
    over = [None] * MODES
    zero = jnp.zeros((1, AGG_DEV), jnp.float32)
    for i in range(MODES):
        square = g[i][i]
        for k in range(i):
            square = square - up[k][i] * up[k][i]
        pivot = jnp.sqrt(square)
        up[i][i] = pivot
        over[i] = 1.0 / pivot
        for j in range(i + 1, MODES):
            rest = g[i][j]
            for k in range(i):
                rest = rest - up[k][i] * up[k][j]
            up[i][j] = rest * over[i]
    inv = [[None] * MODES for _ in range(MODES)]
    for i in range(MODES):
        inv[i][i] = over[i]
        for j in range(i + 1, MODES):
            total = inv[i][i] * up[i][j]
            for k in range(i + 1, j):
                total = total + inv[i][k] * up[k][j]
            inv[i][j] = -total * over[j]
    table_ref[...] = jnp.zeros((48, AGG_DEV), jnp.float32)
    for i in range(MODES):
        for j in range(MODES):
            coarse_ref[i * MODES + j : i * MODES + j + 1, :] = up[i][j] if j >= i else zero
            if j >= i:
                table_ref[i * 8 + j : i * 8 + j + 1, :] = inv[i][j]

    def put(c, total):
        answer_ref[:, c * 128 : (c + 1) * 128] = total
        message_ref[c % 2, MODES * (c // 2) : MODES * (c // 2 + 1), :] = total[0:MODES]

    apply_tables(rows8_ref, landed_ref, table_ref, put)
    for h in range(2):
        send_ref[h * 128 : (h + 1) * 128, :] = message_ref[h].T


def padded_kernel(rows_ref, agg_ref, place_ref, arrive_ref, table_ref, hot_ref, answer_ref, padded_ref, own_ref, left_ref, low_ref):
    def put(c, total):
        own_ref[:, c * 128 : (c + 1) * 128] = total

    apply_tables(rows_ref, hot_ref, table_ref, put)
    for c in range(CHUNKS):
        cols = slice(c * 128, (c + 1) * 128)
        agg = agg_ref[c : c + 1, :]
        slot = jnp.where(agg >= 0, agg * 128 + place_ref[c : c + 1, :], -1)
        high_part(own_ref[:, cols], slot, 32, c, left_ref)
        low_part(slot, c, low_ref)
        landing = of_chunk(arrive_ref, c)
        high_part(answer_ref[:, cols], landing, 32, CHUNKS + c, left_ref)
        low_part(landing, CHUNKS + c, low_ref)
    found = nt_dot(left_ref[...], low_ref[...])
    for a in range(AGG_DEV):
        part = found[(a // 2) * 16 : (a // 2) * 16 + 16, (a % 2) * 128 : (a % 2) * 128 + 128]
        padded_ref[:, a * 128 : (a + 1) * 128] = part[0:MODES] + part[8 : 8 + MODES]


def fine_kernel(recv_ref, sent_ref, own_ref, fine_ref, message_ref, left_ref, low_ref):
    for h in range(2):
        message_ref[h] = recv_ref[h * 128 : (h + 1) * 128, :].T
        for k in range(LANES):
            tile = jnp.concatenate([message_ref[h, MODES * k : MODES * (k + 1), :], jnp.zeros((2, 128), jnp.float32)], axis=0)
            high_part(tile, of_chunk(sent_ref, 2 * k + h), 18, 2 * k + h, left_ref)
            low_part(of_chunk(sent_ref, 2 * k + h), 2 * k + h, low_ref)
    found = nt_dot(left_ref[...], low_ref[...])
    for c in range(CHUNKS):
        cols = slice(c * 128, (c + 1) * 128)
        part = found[(c // 2) * 16 : (c // 2) * 16 + 16, (c % 2) * 128 : (c % 2) * 128 + 128]
        fine_ref[:, cols] = own_ref[0:MODES, cols] + (part[0:MODES] + part[8 : 8 + MODES])


def f32(*shape):
    return jax.ShapeDtypeStruct(shape, jnp.float32)


def i32(*shape):
    return jax.ShapeDtypeStruct(shape, jnp.int32)


def bf16(*shape):
    return jax.ShapeDtypeStruct(shape, jnp.bfloat16)


def vm(*shape):
    return pltpu.VMEM(shape, jnp.float32)


def vb(*shape):
    return pltpu.VMEM(shape, jnp.bfloat16)


def call(kernel, out_shape, scratch, *args, mib, scalar=False, place=pltpu.VMEM):
    specs = [pl.BlockSpec(memory_space=place) for _ in args]
    if scalar:
        specs[0] = pl.BlockSpec(memory_space=pltpu.SMEM)
    many = isinstance(out_shape, tuple)
    one = pl.BlockSpec(memory_space=pltpu.VMEM)
    return pl.pallas_call(
        kernel,
        out_shape=out_shape,
        in_specs=specs,
        out_specs=tuple(one for _ in out_shape) if many else one,
        scratch_shapes=scratch,
        compiler_params=pltpu.CompilerParams(vmem_limit_bytes=mib * 1024 * 1024),
        name=kernel.__name__,
    )(*args)


def exchange(message):
    return lax.all_to_all(message, AXES, 0, 0, tiled=True)


def body(nullspace, owner_device, local_aggregate, position, sent_rows, arrival_slot):
    me = (lax.axis_index("dom") * lax.axis_size("slab") + lax.axis_index("slab")).reshape(1)
    owner = owner_device.reshape(CHUNKS, 128)
    local = local_aggregate.reshape(CHUNKS, 128)
    place = position.reshape(CHUNKS, 128)
    sent = jnp.transpose(sent_rows, (2, 0, 1))
    arrive = jnp.transpose(arrival_slot, (2, 0, 1))
    send = call(
        pick_kernel,
        f32(PEERS, 128),
        [vm(MODES, ROWS), pltpu.VMEM((LANES, 1, PEERS), jnp.int32), vb(144, 768), vm(128, 128), pltpu.SemaphoreType.DMA((2,))],
        pltpu.with_memory_space_constraint(nullspace, pltpu.HBM), pltpu.with_memory_space_constraint(sent, pltpu.HBM),
        mib=4, place=pltpu.HBM,
    )
    recv = exchange(send)
    gram, agg, hot, landed = call(
        own_kernel,
        (f32(48, AGG_DEV), i32(CHUNKS, 128), bf16(AGG_DEV, ROWS), bf16(AGG_DEV, ROWS)),
        [vm(8, ROWS), vb(144, ROWS)],
        me, nullspace, owner, local, arrive, sent,
        mib=6, scalar=True,
    )
    send, coarse, table, answer = call(
        factor_kernel,
        (f32(PEERS, 128), f32(36, AGG_DEV), f32(48, AGG_DEV), f32(8, ROWS)),
        [vm(8, ROWS), vb(144, ROWS), vm(2, 128, 128)],
        recv, landed, gram,
        mib=6,
    )
    recv = exchange(send)
    padded, own = call(
        padded_kernel,
        (f32(MODES, AGG_DEV * PAD), f32(8, ROWS)),
        [vb(512, 2 * ROWS), vb(256, 2 * ROWS)],
        nullspace, agg, place, arrive, table, hot, answer,
        mib=20,
    )
    fine = call(
        fine_kernel,
        f32(MODES, ROWS),
        [vm(2, 128, 128), vb(288, ROWS), vb(256, ROWS)],
        recv, sent, own,
        mib=6,
    )
    return fine, padded, coarse


def solution(mesh):
    in_specs = (
        P(None, AXES),
        P(AXES),
        P(AXES),
        P(AXES),
        P(AXES, None, None),
        P(AXES, None, None),
    )
    out_specs = (P(None, AXES), P(None, AXES), P(None, AXES))
    return jax.shard_map(body, mesh=mesh, in_specs=in_specs, out_specs=out_specs, check_vma=False)
```

time: 59.8 us -> 55.2 us (0.923)
  Pallas kernels: 23.4 us -> 11.9 us
  waiting for transfers between devices: 11.7 us -> 20.2 us
  local copies, waits for them, and re-layouts: 2.36 us -> 0.7 us
    pallas_call x5, Pallas kernels: 23.4 us -> 11.9 us  [call(): pl.pallas_call(kernel, out_shape=out_shape, in_specs=specs, out_specs=tup...]
    all_to_all x2, waiting for transfers between devices: 11.7 us -> 20.2 us  [exchange(): return lax.all_to_all(message, AXES, 0, 0, tiled=True)]
    unnamed x14 -> x12, local copies, waits for them, and re-layouts: 2.35 us -> 0.7 us
  transfers between devices with their start and end apart: 2 -> 2, of which waited for: 2 -> 2; matrix products, arithmetic and copies ran while one was open for 0% -> 0% of each run, Pallas kernels for 23% -> 9%
where the time goes in v2:
time: 55.2 us; the launch traced here: 55 us
  starting transfers between devices  21.3 us (39%)
  waiting for transfers between devices  20.2 us (37%)
  Pallas kernels  11.9 us (22%)
  between operations  0.75 us (1%)
  local copies, waits for them, and re-layouts  0.7 us (1%)
    all_to_all x2, starting transfers between devices, exchange(): return lax.all_to_all(message, AXES, 0, 0, tiled=True)  21.3 us
    all_to_all x2, waiting for transfers between devices, exchange(): return lax.all_to_all(message, AXES, 0, 0, tiled=True)  20.2 us
    pallas_call x5, Pallas kernels, call(): pl.pallas_call(kernel, out_shape=out_shape, in_specs=specs, out_specs=tup...  11.9 us
  transfers between devices with their start and end apart: 2, of which 2 were waited for; matrix products, arithmetic and copies ran while one was open for 0% of the time, Pallas kernels for 9%

profile of v2, /device:TPU:1, one launch (start us, length us, event | category | flops | bytes accessed | tf_op | source)
XLA Modules:
  0.0 55.0 jit_solution(9685865764657243660)
XLA Ops:
  0.6 3.0 %pick_kernel.1 = f32[256,128]{1,0:T(8,128)} custom-call(f32[6,4608]{1,0:T(8,128)} %rows_ref.3, s32[18,1,256]{2,1,0:T(1,128)} %bitcast.16), custom_call_target="tpu_custom_call" | custom-call | tf_op jit(solution)/shard_map/pick_kernel/pallas_call | solution.py:250
  3.6 0.0 copy-start
  3.6 0.0 copy-start.2
  3.6 0.0 copy-start.3
  3.6 0.0 copy-start.4
  3.6 15.7 %all-to-all-start = ((f32[256,1,128]{2,1,0:T(1,128)}), f32[256,1,128]{2,1,0:T(1,128)S(1)}, u32[]{:S(2)}, u32[]{:S(2)}) async-start(f32[256,1,128]{2,1,0:T(1,128)} %bitcast.2), calls=%async_computation | async-start | bytes 262144 | tf_op jit(solution)/shard_map/all_to_all | solution.py:262
  19.3 0.0 copy-start.1
  19.3 0.0 copy-done
  19.3 0.0 copy-done.2
  19.4 0.0 copy-done.3
  19.4 0.0 copy-done.4
  19.4 0.7 %copy-done.1 = s32[1,256,18]{1,0,2:T(1,128)S(1)} copy-done((s32[1,256,18]{1,0,2:T(1,128)S(1)}, s32[1,256,18]{1,0,2:T(1,128)}, u32[]{:S(2)}) %copy-start.1) | copy-done | bytes 18456
  20.0 0.8 %own_kernel.1 = (f32[48,64]{1,0:T(8,128)S(1)}, s32[36,128]{1,0:T(8,128)S(1)}, bf16[64,4608]{1,0:T(8,128)(2,1)S(1)}, bf16[64,4608]{1,0:T(8,128)(2,1)S(1)}) custom-call(s32[1]{0:T(128)} %bitcast.4.me_ref, f32[6,4608]{1,0:T(8,128)S(1)} %copy-done, s32[36,128]{1,0:T(8,128)S(1)} %bitcast.21, s32[36,128]{1,0:T(8,128)S(1)} %bitcast.22, s32[18,1,256]{2,1,0:T(1,128)S(1)} %bitcast.19, ...), custom_call_target="tpu_custom_call" | custom-call | tf_op jit(solution)/shard_map/own_kernel/pallas_call | solution.py:250
  20.8 11.5 %all-to-all-done = f32[256,1,128]{2,1,0:T(1,128)S(1)} async-done(((f32[256,1,128]{2,1,0:T(1,128)}), f32[256,1,128]{2,1,0:T(1,128)S(1)}, u32[]{:S(2)}, u32[]{:S(2)}) %all-to-all-start) | async-done | bytes 131104 | tf_op jit(solution)/shard_map/all_to_all | solution.py:262
  32.3 1.9 %factor_kernel.1 = (f32[256,128]{1,0:T(8,128)}, f32[36,64]{1,0:T(8,128)}, f32[48,64]{1,0:T(8,128)S(1)}, f32[8,4608]{1,0:T(8,128)S(1)}) custom-call(f32[256,128]{1,0:T(8,128)S(1)} %bitcast.15, bf16[64,4608]{1,0:T(8,128)(2,1)S(1)} %get-tuple-element.13.landed_ref, f32[48,64]{1,0:T(8,128)S(1)} %get-tuple-element.14.gram_ref), custom_call_target="tpu_custom_call" | custom-call | tf_op jit(solution)/shard_map/factor_kernel/pallas_call | solution.py:250
  34.2 0.0 copy-start.5
  34.2 5.7 %all-to-all-start.1 = ((f32[256,1,128]{2,1,0:T(1,128)}), f32[256,1,128]{2,1,0:T(1,128)S(1)}, u32[]{:S(2)}, u32[]{:S(2)}) async-start(f32[256,1,128]{2,1,0:T(1,128)} %bitcast.9), calls=%async_computation.1 | async-start | bytes 262144 | tf_op jit(solution)/shard_map/all_to_all | solution.py:262
  39.9 0.0 copy-done.5
  39.9 4.3 %padded_kernel.1 = (f32[6,8192]{1,0:T(8,128)}, f32[8,4608]{1,0:T(8,128)S(1)}) custom-call(f32[6,4608]{1,0:T(8,128)S(1)} %copy-done, s32[36,128]{1,0:T(8,128)S(1)} %get-tuple-element.16.agg_ref, s32[36,128]{1,0:T(8,128)S(1)} %bitcast.23, s32[18,1,256]{2,1,0:T(1,128)S(1)} %bitcast.20, f32[48,64]{1,0:T(8,128)S(1)} %get-tuple-element.17.table_ref, ...), custom_call_target="tpu_custom_call" | custom-call | tf_op jit(solution)/shard_map/padded_kernel/pallas_call | solution.py:250
  44.2 8.8 %all-to-all-done.1 = f32[256,1,128]{2,1,0:T(1,128)S(1)} async-done(((f32[256,1,128]{2,1,0:T(1,128)}), f32[256,1,128]{2,1,0:T(1,128)S(1)}, u32[]{:S(2)}, u32[]{:S(2)}) %all-to-all-start.1) | async-done | bytes 131104 | tf_op jit(solution)/shard_map/all_to_all | solution.py:262
  53.0 1.9 %fine_kernel.1 = f32[6,4608]{1,0:T(8,128)} custom-call(f32[256,128]{1,0:T(8,128)S(1)} %bitcast.14, s32[18,1,256]{2,1,0:T(1,128)S(1)} %bitcast.18, f32[8,4608]{1,0:T(8,128)S(1)} %get-tuple-element.20.own_ref), custom_call_target="tpu_custom_call" | custom-call | tf_op jit(solution)/shard_map/fine_kernel/pallas_call | solution.py:250
Async XLA Ops:
  3.6 15.7 %copy-start = (f32[6,4608]{1,0:T(8,128)S(1)}, f32[6,4608]{1,0:T(8,128)}, u32[]{:S(2)}) copy-start(f32[6,4608]{1,0:T(8,128)} %rows_ref.3) | copy-start | bytes 331780
  3.6 15.7 %copy-start.2 = (s32[1,256,18]{1,0,2:T(1,128)S(1)}, s32[1,256,18]{1,0,2:T(1,128)}, u32[]{:S(2)}) copy-start(s32[1,256,18]{1,0,2:T(1,128)} %param.11) | copy-start | bytes 55300
  3.6 15.7 %copy-start.3 = (s32[4608]{0:T(1024)S(1)}, s32[4608]{0:T(1024)}, u32[]{:S(2)}) copy-start(s32[4608]{0:T(1024)} %param.7) | copy-start | bytes 55300
  3.6 15.7 %copy-start.4 = (s32[4608]{0:T(1024)S(1)}, s32[4608]{0:T(1024)}, u32[]{:S(2)}) copy-start(s32[4608]{0:T(1024)} %param.8) | copy-start | bytes 55300
  3.6 28.6 %all-to-all-start = ((f32[256,1,128]{2,1,0:T(1,128)}), f32[256,1,128]{2,1,0:T(1,128)S(1)}, u32[]{:S(2)}, u32[]{:S(2)}) async-start(f32[256,1,128]{2,1,0:T(1,128)} %bitcast.2), calls=%async_computation | async-start | bytes 262144 | tf_op jit(solution)/shard_map/all_to_all | solution.py:262
  19.3 0.7 %copy-start.1 = (s32[1,256,18]{1,0,2:T(1,128)S(1)}, s32[1,256,18]{1,0,2:T(1,128)}, u32[]{:S(2)}) copy-start(s32[1,256,18]{1,0,2:T(1,128)} %param.10) | copy-start | bytes 55300
  34.2 5.7 %copy-start.5 = (s32[4608]{0:T(1024)S(1)}, s32[4608]{0:T(1024)}, u32[]{:S(2)}) copy-start(s32[4608]{0:T(1024)} %param.9) | copy-start | bytes 55300
  34.2 18.8 %all-to-all-start.1 = ((f32[256,1,128]{2,1,0:T(1,128)}), f32[256,1,128]{2,1,0:T(1,128)S(1)}, u32[]{:S(2)}, u32[]{:S(2)}) async-start(f32[256,1,128]{2,1,0:T(1,128)} %bitcast.9), calls=%async_computation.1 | async-start | bytes 262144 | tf_op jit(solution)/shard_map/all_to_all | solution.py:262

commit v3 on v2

--- a/solution.py
+++ b/solution.py
@@ -41,37 +41,50 @@
     return top, mid, low
 
 
+def split2(value):
+    top = value.astype(jnp.bfloat16)
+    return top, (value - top.astype(jnp.float32)).astype(jnp.bfloat16)
+
+
+def fill_table(tile_of, left_ref):
+    pad = jnp.zeros((2, 128), jnp.float32)
+    for hi in range(0, 18, 2):
+        for side in range(2):
+            pair = jnp.concatenate([tile_of(2 * hi + side), pad, tile_of(2 * hi + side + 2), pad], axis=0)
+            for s, piece in enumerate(split2(pair)):
+                left_ref[hi * 8 : hi * 8 + 16, s * 256 + side * 128 : s * 256 + side * 128 + 128] = piece
+
+
+def gather_chunks(index, left_ref):
+    iota = row_iota((256, 128)).astype(jnp.float32).astype(jnp.bfloat16)
+    hot = jnp.concatenate([one_hot_rows(as_row(v & 255), iota) for v in index], axis=1)
+    found = jnp.dot(left_ref[...], jnp.concatenate([hot, hot], axis=0), preferred_element_type=jnp.float32)
+    result = []
+    for n, v in enumerate(index):
+        tile = jnp.broadcast_to(v >> 8, (8, 128))
+        total = jnp.zeros((8, 128), jnp.float32)
+        for t in range(18):
+            total = jnp.where(tile == t, found[t * 8 : t * 8 + 8, n * 128 : (n + 1) * 128], total)
+        result.append(total)
+    return result
+
+
 def pick_kernel(rows_hbm, sent_hbm, send_ref, rows_ref, sent_ref, left_ref, message_ref, arrived):
     sent_copy = pltpu.make_async_copy(sent_hbm, sent_ref, arrived.at[0])
     rows_copy = pltpu.make_async_copy(rows_hbm, rows_ref, arrived.at[1])
     sent_copy.start()
     rows_copy.start()
     rows_copy.wait()
-    pad = jnp.zeros((2, 128), jnp.float32)
-    for hi in range(0, 18, 2):
-        for side in range(2):
-            t = 2 * hi + side
-            first = rows_ref[:, t * 128 : (t + 1) * 128]
-            second = rows_ref[:, (t + 2) * 128 : (t + 3) * 128]
-            pair = jnp.concatenate([first, pad, second, pad], axis=0)
-            for s, piece in enumerate(split3(pair)):
-                left_ref[hi * 8 : hi * 8 + 16, s * 256 + side * 128 : s * 256 + side * 128 + 128] = piece
+    fill_table(lambda t: rows_ref[:, t * 128 : (t + 1) * 128], left_ref)
     sent_copy.wait()
-    lane_iota = row_iota((256, 128)).astype(jnp.float32).astype(jnp.bfloat16)
     for h in range(2):
-        message_ref[...] = jnp.zeros((128, 128), jnp.float32)
+        message_ref[h, MODES * LANES : 128, :] = jnp.zeros((128 - MODES * LANES, 128), jnp.float32)
         for k0 in range(0, LANES, 2):
             index = [sent_ref[k, :, h * 128 : (h + 1) * 128] for k in range(k0, k0 + 2)]
-            hot = jnp.concatenate([one_hot_rows(as_row(v & 255), lane_iota) for v in index], axis=1)
-            found = jnp.dot(left_ref[...], jnp.concatenate([hot] * 3, axis=0), preferred_element_type=jnp.float32)
-            for n, v in enumerate(index):
-                tile = jnp.broadcast_to(v >> 8, (8, 128))
-                total = jnp.zeros((8, 128), jnp.float32)
-                for t in range(18):
-                    total = jnp.where(tile == t, found[t * 8 : t * 8 + 8, n * 128 : (n + 1) * 128], total)
+            for n, total in enumerate(gather_chunks(index, left_ref)):
                 k = k0 + n
-                message_ref[MODES * k : MODES * (k + 1), :] = total[0:MODES]
-        send_ref[h * 128 : (h + 1) * 128, :] = message_ref[...].T
+                message_ref[h, MODES * k : MODES * (k + 1), :] = total[0:MODES]
+        send_ref[h * 128 : (h + 1) * 128, :] = message_ref[h].T
 
 
 def gram_part(rows8_ref, hot_ref, left_ref):
@@ -97,16 +110,28 @@
     return table_ref[c // 2, :, (c % 2) * 128 : (c % 2) * 128 + 128]
 
 
-def own_kernel(me_ref, rows_ref, owner_ref, local_ref, arrive_ref, sent_ref, gram_ref, agg_ref, hot_ref, landed_ref,
-               rows8_ref, left_ref):
+def own_kernel(me_ref, rows_ref, owner_ref, local_ref, arrive_ref, sent_ref, gram_ref, agg_ref, hot_ref, landed_ref, source_ref,
+               rows8_ref, left_ref, code_ref, low_ref):
     owned = owner_ref[...] == me_ref[0]
     agg_ref[...] = jnp.where(owned, local_ref[...], -1)
     rows8_ref[0:MODES, :] = rows_ref[...]
     rows8_ref[MODES:8, :] = jnp.zeros((2, ROWS), jnp.float32)
+    lanes = jnp.broadcast_to(as_row(lax.broadcasted_iota(jnp.int32, (1, 128), 1)), (48, 128))
+    high_iota = row_iota((48, 128)).astype(jnp.float32).astype(jnp.bfloat16)
+    low_iota = row_iota((128, 128)).astype(jnp.float32).astype(jnp.bfloat16)
     for c in range(CHUNKS):
+        cols = slice(c * 128, (c + 1) * 128)
         hot_aggregates(agg_ref[c : c + 1, :], c, hot_ref)
         hot_aggregates(of_chunk(arrive_ref, c) >> 7, c, landed_ref)
+        sent = of_chunk(sent_ref, c)
+        high = as_row(sent >> 7)
+        code_ref[0:48, cols] = one_hot_rows(high, high_iota, jnp.full_like(high_iota, c))
+        code_ref[48:96, cols] = one_hot_rows(high, high_iota, lanes)
+        low_ref[:, cols] = one_hot_rows(as_row(sent & 127), low_iota)
     gram_ref[...] = gram_part(rows8_ref, hot_ref, left_ref)
+    code = nt_dot(code_ref[...], low_ref[...])
+    slot = (code[0:CHUNKS] * 128.0 + code[48 : 48 + CHUNKS]).astype(jnp.int32)
+    source_ref[...] = jnp.where(owned, -1, slot)
 
 
 def apply_tables(rows8_ref, hot_ref, table_ref, put):
@@ -207,18 +232,15 @@
         padded_ref[:, a * 128 : (a + 1) * 128] = part[0:MODES] + part[8 : 8 + MODES]
 
 
-def fine_kernel(recv_ref, sent_ref, own_ref, fine_ref, message_ref, left_ref, low_ref):
+def fine_kernel(recv_ref, source_ref, own_ref, fine_ref, message_ref, left_ref):
     for h in range(2):
         message_ref[h] = recv_ref[h * 128 : (h + 1) * 128, :].T
-        for k in range(LANES):
-            tile = jnp.concatenate([message_ref[h, MODES * k : MODES * (k + 1), :], jnp.zeros((2, 128), jnp.float32)], axis=0)
-            high_part(tile, of_chunk(sent_ref, 2 * k + h), 18, 2 * k + h, left_ref)
-            low_part(of_chunk(sent_ref, 2 * k + h), 2 * k + h, low_ref)
-    found = nt_dot(left_ref[...], low_ref[...])
-    for c in range(CHUNKS):
-        cols = slice(c * 128, (c + 1) * 128)
-        part = found[(c // 2) * 16 : (c // 2) * 16 + 16, (c % 2) * 128 : (c % 2) * 128 + 128]
-        fine_ref[:, cols] = own_ref[0:MODES, cols] + (part[0:MODES] + part[8 : 8 + MODES])
+    fill_table(lambda t: message_ref[t % 2, MODES * (t // 2) : MODES * (t // 2 + 1), :], left_ref)
+    for c0 in range(0, CHUNKS, 2):
+        index = [source_ref[c : c + 1, :] for c in range(c0, c0 + 2)]
+        for n, total in enumerate(gather_chunks(index, left_ref)):
+            cols = slice((c0 + n) * 128, (c0 + n + 1) * 128)
+            fine_ref[:, cols] = own_ref[0:MODES, cols] + total[0:MODES]
 
 
 def f32(*shape):
@@ -272,17 +294,17 @@
     send = call(
         pick_kernel,
         f32(PEERS, 128),
-        [vm(MODES, ROWS), pltpu.VMEM((LANES, 1, PEERS), jnp.int32), vb(144, 768), vm(128, 128), pltpu.SemaphoreType.DMA((2,))],
+        [vm(MODES, ROWS), pltpu.VMEM((LANES, 1, PEERS), jnp.int32), vb(144, 512), vm(2, 128, 128), pltpu.SemaphoreType.DMA((2,))],
         pltpu.with_memory_space_constraint(nullspace, pltpu.HBM), pltpu.with_memory_space_constraint(sent, pltpu.HBM),
         mib=4, place=pltpu.HBM,
     )
     recv = exchange(send)
-    gram, agg, hot, landed = call(
+    gram, agg, hot, landed, source = call(
         own_kernel,
-        (f32(48, AGG_DEV), i32(CHUNKS, 128), bf16(AGG_DEV, ROWS), bf16(AGG_DEV, ROWS)),
-        [vm(8, ROWS), vb(144, ROWS)],
+        (f32(48, AGG_DEV), i32(CHUNKS, 128), bf16(AGG_DEV, ROWS), bf16(AGG_DEV, ROWS), i32(CHUNKS, 128)),
+        [vm(8, ROWS), vb(144, ROWS), vb(96, ROWS), vb(128, ROWS)],
         me, nullspace, owner, local, arrive, sent,
-        mib=6, scalar=True,
+        mib=10, scalar=True,
     )
     send, coarse, table, answer = call(
         factor_kernel,
@@ -302,8 +324,8 @@
     fine = call(
         fine_kernel,
         f32(MODES, ROWS),
-        [vm(2, 128, 128), vb(288, ROWS), vb(256, ROWS)],
-        recv, sent, own,
+        [vm(2, 128, 128), vb(144, 512)],
+        recv, source, own,
         mib=6,
     )
     return fine, padded, coarse

time: 55.2 us -> 54.5 us (0.987)
  transfers between devices with their start and end apart: 2 -> 2, of which waited for: 2 -> 2; matrix products, arithmetic and copies ran while one was open for 0% -> 0% of each run, Pallas kernels for 9% -> 10%
where the time goes in v3:
time: 54.5 us; the launch traced here: 54.2 us
  starting transfers between devices  21.3 us (39%)
  waiting for transfers between devices  19.8 us (36%)
  Pallas kernels  11.6 us (21%)
  between operations  0.75 us (1%)
  local copies, waits for them, and re-layouts  0.7 us (1%)
    all_to_all x2, starting transfers between devices, exchange(): return lax.all_to_all(message, AXES, 0, 0, tiled=True)  21.3 us
    all_to_all x2, waiting for transfers between devices, exchange(): return lax.all_to_all(message, AXES, 0, 0, tiled=True)  19.8 us
    pallas_call x5, Pallas kernels, call(): pl.pallas_call(kernel, out_shape=out_shape, in_specs=specs, out_specs=tup...  11.6 us
  transfers between devices with their start and end apart: 2, of which 2 were waited for; matrix products, arithmetic and copies ran while one was open for 0% of the time, Pallas kernels for 10%

profile of v3, /device:TPU:1, one launch (start us, length us, event | category | flops | bytes accessed | tf_op | source)
XLA Modules:
  0.0 54.2 jit_solution(12624504471805921795)
XLA Ops:
  0.6 2.6 %pick_kernel.1 = f32[256,128]{1,0:T(8,128)} custom-call(f32[6,4608]{1,0:T(8,128)} %rows_ref.3, s32[18,1,256]{2,1,0:T(1,128)} %bitcast.16), custom_call_target="tpu_custom_call" | custom-call | tf_op jit(solution)/shard_map/pick_kernel/pallas_call | solution.py:272
  3.2 0.0 copy-start
  3.2 0.0 copy-start.2
  3.3 0.0 copy-start.3
  3.3 0.0 copy-start.4
  3.3 15.7 %all-to-all-start = ((f32[256,1,128]{2,1,0:T(1,128)}), f32[256,1,128]{2,1,0:T(1,128)S(1)}, u32[]{:S(2)}, u32[]{:S(2)}) async-start(f32[256,1,128]{2,1,0:T(1,128)} %bitcast.2), calls=%async_computation | async-start | bytes 262144 | tf_op jit(solution)/shard_map/all_to_all | solution.py:284
  19.0 0.0 copy-start.1
  19.0 0.0 copy-done
  19.0 0.0 copy-done.2
  19.0 0.0 copy-done.3
  19.0 0.0 copy-done.4
  19.0 0.7 %copy-done.1 = s32[1,256,18]{1,0,2:T(1,128)S(1)} copy-done((s32[1,256,18]{1,0,2:T(1,128)S(1)}, s32[1,256,18]{1,0,2:T(1,128)}, u32[]{:S(2)}) %copy-start.1) | copy-done | bytes 18456
  19.7 1.2 %own_kernel.1 = (f32[48,64]{1,0:T(8,128)S(1)}, s32[36,128]{1,0:T(8,128)S(1)}, bf16[64,4608]{1,0:T(8,128)(2,1)S(1)}, bf16[64,4608]{1,0:T(8,128)(2,1)S(1)}, s32[36,128]{1,0:T(8,128)S(1)}) custom-call(s32[1]{0:T(128)} %bitcast.4.me_ref, f32[6,4608]{1,0:T(8,128)S(1)} %copy-done, s32[36,128]{1,0:T(8,128)S(1)} %bitcast.20, s32[36,128]{1,0:T(8,128)S(1)} %bitcast.21, ...), custom_call_target="tpu_custom_call" | custom-call | tf_op jit(solution)/shard_map/own_kernel/pallas_call | solution.py:272
  20.9 11.0 %all-to-all-done = f32[256,1,128]{2,1,0:T(1,128)S(1)} async-done(((f32[256,1,128]{2,1,0:T(1,128)}), f32[256,1,128]{2,1,0:T(1,128)S(1)}, u32[]{:S(2)}, u32[]{:S(2)}) %all-to-all-start) | async-done | bytes 131104 | tf_op jit(solution)/shard_map/all_to_all | solution.py:284
  31.9 1.9 %factor_kernel.1 = (f32[256,128]{1,0:T(8,128)}, f32[36,64]{1,0:T(8,128)}, f32[48,64]{1,0:T(8,128)S(1)}, f32[8,4608]{1,0:T(8,128)S(1)}) custom-call(f32[256,128]{1,0:T(8,128)S(1)} %bitcast.15, bf16[64,4608]{1,0:T(8,128)(2,1)S(1)} %get-tuple-element.14.landed_ref, f32[48,64]{1,0:T(8,128)S(1)} %get-tuple-element.15.gram_ref), custom_call_target="tpu_custom_call" | custom-call | tf_op jit(solution)/shard_map/factor_kernel/pallas_call | solution.py:272
  33.9 0.0 copy-start.5
  33.9 5.7 %all-to-all-start.1 = ((f32[256,1,128]{2,1,0:T(1,128)}), f32[256,1,128]{2,1,0:T(1,128)S(1)}, u32[]{:S(2)}, u32[]{:S(2)}) async-start(f32[256,1,128]{2,1,0:T(1,128)} %bitcast.9), calls=%async_computation.1 | async-start | bytes 262144 | tf_op jit(solution)/shard_map/all_to_all | solution.py:284
  39.5 0.0 copy-done.5
  39.6 4.3 %padded_kernel.1 = (f32[6,8192]{1,0:T(8,128)}, f32[8,4608]{1,0:T(8,128)S(1)}) custom-call(f32[6,4608]{1,0:T(8,128)S(1)} %copy-done, s32[36,128]{1,0:T(8,128)S(1)} %get-tuple-element.18.agg_ref, s32[36,128]{1,0:T(8,128)S(1)} %bitcast.22, s32[18,1,256]{2,1,0:T(1,128)S(1)} %bitcast.19, f32[48,64]{1,0:T(8,128)S(1)} %get-tuple-element.19.table_ref, ...), custom_call_target="tpu_custom_call" | custom-call | tf_op jit(solution)/shard_map/padded_kernel/pallas_call | solution.py:272
  43.9 8.8 %all-to-all-done.1 = f32[256,1,128]{2,1,0:T(1,128)S(1)} async-done(((f32[256,1,128]{2,1,0:T(1,128)}), f32[256,1,128]{2,1,0:T(1,128)S(1)}, u32[]{:S(2)}, u32[]{:S(2)}) %all-to-all-start.1) | async-done | bytes 131104 | tf_op jit(solution)/shard_map/all_to_all | solution.py:284
  52.7 1.6 %fine_kernel.1 = f32[6,4608]{1,0:T(8,128)} custom-call(f32[256,128]{1,0:T(8,128)S(1)} %bitcast.14, s32[36,128]{1,0:T(8,128)S(1)} %get-tuple-element.17.source_ref, f32[8,4608]{1,0:T(8,128)S(1)} %get-tuple-element.22.own_ref), custom_call_target="tpu_custom_call" | custom-call | tf_op jit(solution)/shard_map/fine_kernel/pallas_call | solution.py:272
Async XLA Ops:
  3.2 15.7 %copy-start = (f32[6,4608]{1,0:T(8,128)S(1)}, f32[6,4608]{1,0:T(8,128)}, u32[]{:S(2)}) copy-start(f32[6,4608]{1,0:T(8,128)} %rows_ref.3) | copy-start | bytes 331780
  3.2 15.7 %copy-start.2 = (s32[1,256,18]{1,0,2:T(1,128)S(1)}, s32[1,256,18]{1,0,2:T(1,128)}, u32[]{:S(2)}) copy-start(s32[1,256,18]{1,0,2:T(1,128)} %param.11) | copy-start | bytes 55300
  3.3 15.7 %copy-start.3 = (s32[4608]{0:T(1024)S(1)}, s32[4608]{0:T(1024)}, u32[]{:S(2)}) copy-start(s32[4608]{0:T(1024)} %param.7) | copy-start | bytes 55300
  3.3 15.7 %copy-start.4 = (s32[4608]{0:T(1024)S(1)}, s32[4608]{0:T(1024)}, u32[]{:S(2)}) copy-start(s32[4608]{0:T(1024)} %param.8) | copy-start | bytes 55300
  3.3 28.6 %all-to-all-start = ((f32[256,1,128]{2,1,0:T(1,128)}), f32[256,1,128]{2,1,0:T(1,128)S(1)}, u32[]{:S(2)}, u32[]{:S(2)}) async-start(f32[256,1,128]{2,1,0:T(1,128)} %bitcast.2), calls=%async_computation | async-start | bytes 262144 | tf_op jit(solution)/shard_map/all_to_all | solution.py:284
  19.0 0.7 %copy-start.1 = (s32[1,256,18]{1,0,2:T(1,128)S(1)}, s32[1,256,18]{1,0,2:T(1,128)}, u32[]{:S(2)}) copy-start(s32[1,256,18]{1,0,2:T(1,128)} %param.10) | copy-start | bytes 55300
  33.9 5.7 %copy-start.5 = (s32[4608]{0:T(1024)S(1)}, s32[4608]{0:T(1024)}, u32[]{:S(2)}) copy-start(s32[4608]{0:T(1024)} %param.9) | copy-start | bytes 55300
  33.9 18.8 %all-to-all-start.1 = ((f32[256,1,128]{2,1,0:T(1,128)}), f32[256,1,128]{2,1,0:T(1,128)S(1)}, u32[]{:S(2)}, u32[]{:S(2)}) async-start(f32[256,1,128]{2,1,0:T(1,128)} %bitcast.9), calls=%async_computation.1 | async-start | bytes 262144 | tf_op jit(solution)/shard_map/all_to_all | solution.py:284

commit v4 on v3

--- a/solution.py
+++ b/solution.py
@@ -87,18 +87,21 @@
         send_ref[h * 128 : (h + 1) * 128, :] = message_ref[h].T
 
 
-def gram_part(rows8_ref, hot_ref, left_ref):
+def gram_part(rows_ref, hot_ref, left_ref):
     for c in range(CHUNKS):
         cols = slice(c * 128, (c + 1) * 128)
-        x = rows8_ref[:, cols]
-        for i in range(0, MODES, 2):
-            one = jnp.broadcast_to(rows8_ref[i : i + 1, cols], (8, 128))
-            two = jnp.broadcast_to(rows8_ref[i + 1 : i + 2, cols], (8, 128))
-            pieces = split3(jnp.concatenate([x * one, x * two], axis=0))
+        x = rows_ref[0:8, cols]
+        for d in range(0, 4, 2):
+            pieces = split3(jnp.concatenate([x * rows_ref[d : d + 8, cols], x * rows_ref[d + 1 : d + 9, cols]], axis=0))
             for s in range(3):
-                left_ref[s * 48 + i * 8 : s * 48 + i * 8 + 16, cols] = pieces[s]
+                left_ref[s * 32 + d * 8 : s * 32 + d * 8 + 16, cols] = pieces[s]
     full = nt_dot(left_ref[...], hot_ref[...])
-    return full[0:48] + (full[48:96] + full[96:144])
+    return full[0:32] + (full[32:64] + full[64:96])
+
+
+def gram_row(i, j):
+    d = (j - i) % MODES
+    return 8 * d + i if d <= 3 else 8 * (MODES - d) + j
 
 
 def hot_aggregates(agg_row, c, hot_ref):
@@ -111,11 +114,11 @@
 
 
 def own_kernel(me_ref, rows_ref, owner_ref, local_ref, arrive_ref, sent_ref, gram_ref, agg_ref, hot_ref, landed_ref, source_ref,
-               rows8_ref, left_ref, code_ref, low_ref):
+               twice_ref, left_ref, code_ref, low_ref):
     owned = owner_ref[...] == me_ref[0]
     agg_ref[...] = jnp.where(owned, local_ref[...], -1)
-    rows8_ref[0:MODES, :] = rows_ref[...]
-    rows8_ref[MODES:8, :] = jnp.zeros((2, ROWS), jnp.float32)
+    twice_ref[0:MODES, :] = rows_ref[...]
+    twice_ref[MODES : 2 * MODES, :] = rows_ref[...]
     lanes = jnp.broadcast_to(as_row(lax.broadcasted_iota(jnp.int32, (1, 128), 1)), (48, 128))
     high_iota = row_iota((48, 128)).astype(jnp.float32).astype(jnp.bfloat16)
     low_iota = row_iota((128, 128)).astype(jnp.float32).astype(jnp.bfloat16)
@@ -128,13 +131,13 @@
         code_ref[0:48, cols] = one_hot_rows(high, high_iota, jnp.full_like(high_iota, c))
         code_ref[48:96, cols] = one_hot_rows(high, high_iota, lanes)
         low_ref[:, cols] = one_hot_rows(as_row(sent & 127), low_iota)
-    gram_ref[...] = gram_part(rows8_ref, hot_ref, left_ref)
+    gram_ref[...] = gram_part(twice_ref, hot_ref, left_ref)
     code = nt_dot(code_ref[...], low_ref[...])
     slot = (code[0:CHUNKS] * 128.0 + code[48 : 48 + CHUNKS]).astype(jnp.int32)
     source_ref[...] = jnp.where(owned, -1, slot)
 
 
-def apply_tables(rows8_ref, hot_ref, table_ref, put):
+def apply_tables(rows_ref, hot_ref, table_ref, put):
     table = jnp.concatenate(split3(table_ref[...]), axis=1)
     step = 2
     for c0 in range(0, CHUNKS, step):
@@ -143,9 +146,9 @@
         for c in range(c0, c0 + step):
             cols = slice(c * 128, (c + 1) * 128)
             part = entry[:, (c - c0) * 128 : (c - c0 + 1) * 128]
-            total = jnp.broadcast_to(rows8_ref[0:1, cols], (8, 128)) * part[0:8]
+            total = jnp.broadcast_to(rows_ref[0:1, cols], (8, 128)) * part[0:8]
             for i in range(1, MODES):
-                total = total + jnp.broadcast_to(rows8_ref[i : i + 1, cols], (8, 128)) * part[i * 8 : i * 8 + 8]
+                total = total + jnp.broadcast_to(rows_ref[i : i + 1, cols], (8, 128)) * part[i * 8 : i * 8 + 8]
             put(c, total)
 
 
@@ -164,15 +167,16 @@
 
 
 def factor_kernel(recv_ref, landed_ref, gram_ref, send_ref, coarse_ref, table_ref, answer_ref,
-                  rows8_ref, left_ref, message_ref):
-    rows8_ref[MODES:8, :] = jnp.zeros((2, ROWS), jnp.float32)
+                  twice_ref, left_ref, message_ref):
     for h in range(2):
         message_ref[h] = recv_ref[h * 128 : (h + 1) * 128, :].T
         for k in range(LANES):
             c = 2 * k + h
-            rows8_ref[0:MODES, c * 128 : (c + 1) * 128] = message_ref[h, MODES * k : MODES * (k + 1), :]
-    gram = gram_ref[...] + gram_part(rows8_ref, landed_ref, left_ref)
-    g = [[gram[i * 8 + j : i * 8 + j + 1, :] for j in range(MODES)] for i in range(MODES)]
+            tile = message_ref[h, MODES * k : MODES * (k + 1), :]
+            twice_ref[0:MODES, c * 128 : (c + 1) * 128] = tile
+            twice_ref[MODES : 2 * MODES, c * 128 : (c + 1) * 128] = tile
+    gram = gram_ref[...] + gram_part(twice_ref, landed_ref, left_ref)
+    g = [[gram[gram_row(i, j) : gram_row(i, j) + 1, :] for j in range(MODES)] for i in range(MODES)]
     up = [[None] * MODES for _ in range(MODES)]
     over = [None] * MODES
     zero = jnp.zeros((1, AGG_DEV), jnp.float32)
@@ -207,7 +211,7 @@
         answer_ref[:, c * 128 : (c + 1) * 128] = total
         message_ref[c % 2, MODES * (c // 2) : MODES * (c // 2 + 1), :] = total[0:MODES]
 
-    apply_tables(rows8_ref, landed_ref, table_ref, put)
+    apply_tables(twice_ref, landed_ref, table_ref, put)
     for h in range(2):
         send_ref[h * 128 : (h + 1) * 128, :] = message_ref[h].T
 
@@ -301,15 +305,15 @@
     recv = exchange(send)
     gram, agg, hot, landed, source = call(
         own_kernel,
-        (f32(48, AGG_DEV), i32(CHUNKS, 128), bf16(AGG_DEV, ROWS), bf16(AGG_DEV, ROWS), i32(CHUNKS, 128)),
-        [vm(8, ROWS), vb(144, ROWS), vb(96, ROWS), vb(128, ROWS)],
+        (f32(32, AGG_DEV), i32(CHUNKS, 128), bf16(AGG_DEV, ROWS), bf16(AGG_DEV, ROWS), i32(CHUNKS, 128)),
+        [vm(12, ROWS), vb(96, ROWS), vb(96, ROWS), vb(128, ROWS)],
         me, nullspace, owner, local, arrive, sent,
         mib=10, scalar=True,
     )
     send, coarse, table, answer = call(
         factor_kernel,
         (f32(PEERS, 128), f32(36, AGG_DEV), f32(48, AGG_DEV), f32(8, ROWS)),
-        [vm(8, ROWS), vb(144, ROWS), vm(2, 128, 128)],
+        [vm(12, ROWS), vb(96, ROWS), vm(2, 128, 128)],
         recv, landed, gram,
         mib=6,
     )

time: 54.5 us -> 54.5 us (level)
  no operation moved by 1% of the time
where the time goes in v4:
time: 54.5 us; the launch traced here: 54.2 us
  starting transfers between devices  21.3 us (39%)
  waiting for transfers between devices  19.9 us (37%)
  Pallas kernels  11.5 us (21%)
  between operations  0.75 us (1%)
  local copies, waits for them, and re-layouts  0.7 us (1%)
    all_to_all x2, starting transfers between devices, exchange(): return lax.all_to_all(message, AXES, 0, 0, tiled=True)  21.3 us
    all_to_all x2, waiting for transfers between devices, exchange(): return lax.all_to_all(message, AXES, 0, 0, tiled=True)  19.9 us
    pallas_call x5, Pallas kernels, call(): pl.pallas_call(kernel, out_shape=out_shape, in_specs=specs, out_specs=tup...  11.5 us
  transfers between devices with their start and end apart: 2, of which 2 were waited for; matrix products, arithmetic and copies ran while one was open for 0% of the time, Pallas kernels for 10%

profile of v4, /device:TPU:1, one launch (start us, length us, event | category | flops | bytes accessed | tf_op | source)
XLA Modules:
  0.0 54.2 jit_solution(13463199253170198102)
XLA Ops:
  0.6 2.6 %pick_kernel.1 = f32[256,128]{1,0:T(8,128)} custom-call(f32[6,4608]{1,0:T(8,128)} %rows_ref.3, s32[18,1,256]{2,1,0:T(1,128)} %bitcast.16), custom_call_target="tpu_custom_call" | custom-call | tf_op jit(solution)/shard_map/pick_kernel/pallas_call | solution.py:276
  3.2 0.0 copy-start
  3.2 0.0 copy-start.2
  3.3 0.0 copy-start.3
  3.3 0.0 copy-start.4
  3.3 15.7 %all-to-all-start = ((f32[256,1,128]{2,1,0:T(1,128)}), f32[256,1,128]{2,1,0:T(1,128)S(1)}, u32[]{:S(2)}, u32[]{:S(2)}) async-start(f32[256,1,128]{2,1,0:T(1,128)} %bitcast.2), calls=%async_computation | async-start | bytes 262144 | tf_op jit(solution)/shard_map/all_to_all | solution.py:288
  19.0 0.0 copy-start.1
  19.0 0.0 copy-done
  19.0 0.0 copy-done.2
  19.0 0.0 copy-done.3
  19.0 0.0 copy-done.4
  19.0 0.7 %copy-done.1 = s32[1,256,18]{1,0,2:T(1,128)S(1)} copy-done((s32[1,256,18]{1,0,2:T(1,128)S(1)}, s32[1,256,18]{1,0,2:T(1,128)}, u32[]{:S(2)}) %copy-start.1) | copy-done | bytes 18456
  19.7 1.2 %own_kernel.1 = (f32[32,64]{1,0:T(8,128)S(1)}, s32[36,128]{1,0:T(8,128)S(1)}, bf16[64,4608]{1,0:T(8,128)(2,1)S(1)}, bf16[64,4608]{1,0:T(8,128)(2,1)S(1)}, s32[36,128]{1,0:T(8,128)S(1)}) custom-call(s32[1]{0:T(128)} %bitcast.4.me_ref, f32[6,4608]{1,0:T(8,128)S(1)} %copy-done, s32[36,128]{1,0:T(8,128)S(1)} %bitcast.20, s32[36,128]{1,0:T(8,128)S(1)} %bitcast.21, ...), custom_call_target="tpu_custom_call" | custom-call | tf_op jit(solution)/shard_map/own_kernel/pallas_call | solution.py:276
  20.9 11.1 %all-to-all-done = f32[256,1,128]{2,1,0:T(1,128)S(1)} async-done(((f32[256,1,128]{2,1,0:T(1,128)}), f32[256,1,128]{2,1,0:T(1,128)S(1)}, u32[]{:S(2)}, u32[]{:S(2)}) %all-to-all-start) | async-done | bytes 131104 | tf_op jit(solution)/shard_map/all_to_all | solution.py:288
  31.9 1.9 %factor_kernel.1 = (f32[256,128]{1,0:T(8,128)}, f32[36,64]{1,0:T(8,128)}, f32[48,64]{1,0:T(8,128)S(1)}, f32[8,4608]{1,0:T(8,128)S(1)}) custom-call(f32[256,128]{1,0:T(8,128)S(1)} %bitcast.15, bf16[64,4608]{1,0:T(8,128)(2,1)S(1)} %get-tuple-element.14.landed_ref, f32[32,64]{1,0:T(8,128)S(1)} %get-tuple-element.15.gram_ref), custom_call_target="tpu_custom_call" | custom-call | tf_op jit(solution)/shard_map/factor_kernel/pallas_call | solution.py:276
  33.8 0.0 copy-start.5
  33.8 5.7 %all-to-all-start.1 = ((f32[256,1,128]{2,1,0:T(1,128)}), f32[256,1,128]{2,1,0:T(1,128)S(1)}, u32[]{:S(2)}, u32[]{:S(2)}) async-start(f32[256,1,128]{2,1,0:T(1,128)} %bitcast.9), calls=%async_computation.1 | async-start | bytes 262144 | tf_op jit(solution)/shard_map/all_to_all | solution.py:288
  39.5 0.0 copy-done.5
  39.5 4.3 %padded_kernel.1 = (f32[6,8192]{1,0:T(8,128)}, f32[8,4608]{1,0:T(8,128)S(1)}) custom-call(f32[6,4608]{1,0:T(8,128)S(1)} %copy-done, s32[36,128]{1,0:T(8,128)S(1)} %get-tuple-element.18.agg_ref, s32[36,128]{1,0:T(8,128)S(1)} %bitcast.22, s32[18,1,256]{2,1,0:T(1,128)S(1)} %bitcast.19, f32[48,64]{1,0:T(8,128)S(1)} %get-tuple-element.19.table_ref, ...), custom_call_target="tpu_custom_call" | custom-call | tf_op jit(solution)/shard_map/padded_kernel/pallas_call | solution.py:276
  43.8 8.8 %all-to-all-done.1 = f32[256,1,128]{2,1,0:T(1,128)S(1)} async-done(((f32[256,1,128]{2,1,0:T(1,128)}), f32[256,1,128]{2,1,0:T(1,128)S(1)}, u32[]{:S(2)}, u32[]{:S(2)}) %all-to-all-start.1) | async-done | bytes 131104 | tf_op jit(solution)/shard_map/all_to_all | solution.py:288
  52.6 1.6 %fine_kernel.1 = f32[6,4608]{1,0:T(8,128)} custom-call(f32[256,128]{1,0:T(8,128)S(1)} %bitcast.14, s32[36,128]{1,0:T(8,128)S(1)} %get-tuple-element.17.source_ref, f32[8,4608]{1,0:T(8,128)S(1)} %get-tuple-element.22.own_ref), custom_call_target="tpu_custom_call" | custom-call | tf_op jit(solution)/shard_map/fine_kernel/pallas_call | solution.py:276
Async XLA Ops:
  3.2 15.7 %copy-start = (f32[6,4608]{1,0:T(8,128)S(1)}, f32[6,4608]{1,0:T(8,128)}, u32[]{:S(2)}) copy-start(f32[6,4608]{1,0:T(8,128)} %rows_ref.3) | copy-start | bytes 331780
  3.2 15.7 %copy-start.2 = (s32[1,256,18]{1,0,2:T(1,128)S(1)}, s32[1,256,18]{1,0,2:T(1,128)}, u32[]{:S(2)}) copy-start(s32[1,256,18]{1,0,2:T(1,128)} %param.11) | copy-start | bytes 55300
  3.3 15.7 %copy-start.3 = (s32[4608]{0:T(1024)S(1)}, s32[4608]{0:T(1024)}, u32[]{:S(2)}) copy-start(s32[4608]{0:T(1024)} %param.7) | copy-start | bytes 55300
  3.3 15.7 %copy-start.4 = (s32[4608]{0:T(1024)S(1)}, s32[4608]{0:T(1024)}, u32[]{:S(2)}) copy-start(s32[4608]{0:T(1024)} %param.8) | copy-start | bytes 55300
  3.3 28.6 %all-to-all-start = ((f32[256,1,128]{2,1,0:T(1,128)}), f32[256,1,128]{2,1,0:T(1,128)S(1)}, u32[]{:S(2)}, u32[]{:S(2)}) async-start(f32[256,1,128]{2,1,0:T(1,128)} %bitcast.2), calls=%async_computation | async-start | bytes 262144 | tf_op jit(solution)/shard_map/all_to_all | solution.py:288
  19.0 0.7 %copy-start.1 = (s32[1,256,18]{1,0,2:T(1,128)S(1)}, s32[1,256,18]{1,0,2:T(1,128)}, u32[]{:S(2)}) copy-start(s32[1,256,18]{1,0,2:T(1,128)} %param.10) | copy-start | bytes 55300
  33.8 5.7 %copy-start.5 = (s32[4608]{0:T(1024)S(1)}, s32[4608]{0:T(1024)}, u32[]{:S(2)}) copy-start(s32[4608]{0:T(1024)} %param.9) | copy-start | bytes 55300
  33.8 18.8 %all-to-all-start.1 = ((f32[256,1,128]{2,1,0:T(1,128)}), f32[256,1,128]{2,1,0:T(1,128)S(1)}, u32[]{:S(2)}, u32[]{:S(2)}) async-start(f32[256,1,128]{2,1,0:T(1,128)} %bitcast.9), calls=%async_computation.1 | async-start | bytes 262144 | tf_op jit(solution)/shard_map/all_to_all | solution.py:288

commit v5 on v4

--- a/solution.py
+++ b/solution.py
@@ -71,10 +71,13 @@
 
 def pick_kernel(rows_hbm, sent_hbm, send_ref, rows_ref, sent_ref, left_ref, message_ref, arrived):
     sent_copy = pltpu.make_async_copy(sent_hbm, sent_ref, arrived.at[0])
-    rows_copy = pltpu.make_async_copy(rows_hbm, rows_ref, arrived.at[1])
+    parts = [pl.ds(n * 1152, 1152) for n in range(4)]
+    rows_copies = [pltpu.make_async_copy(rows_hbm.at[:, part], rows_ref.at[:, part], arrived.at[1 + n]) for n, part in enumerate(parts)]
     sent_copy.start()
-    rows_copy.start()
-    rows_copy.wait()
+    for copy in rows_copies:
+        copy.start()
+    for copy in rows_copies:
+        copy.wait()
     fill_table(lambda t: rows_ref[:, t * 128 : (t + 1) * 128], left_ref)
     sent_copy.wait()
     for h in range(2):
@@ -139,7 +142,7 @@
 
 def apply_tables(rows_ref, hot_ref, table_ref, put):
     table = jnp.concatenate(split3(table_ref[...]), axis=1)
-    step = 2
+    step = 6
     for c0 in range(0, CHUNKS, step):
         hot = hot_ref[:, c0 * 128 : (c0 + step) * 128]
         entry = jnp.dot(table, jnp.concatenate([hot] * 3, axis=0), preferred_element_type=jnp.float32)
@@ -298,7 +301,7 @@
     send = call(
         pick_kernel,
         f32(PEERS, 128),
-        [vm(MODES, ROWS), pltpu.VMEM((LANES, 1, PEERS), jnp.int32), vb(144, 512), vm(2, 128, 128), pltpu.SemaphoreType.DMA((2,))],
+        [vm(MODES, ROWS), pltpu.VMEM((LANES, 1, PEERS), jnp.int32), vb(144, 512), vm(2, 128, 128), pltpu.SemaphoreType.DMA((5,))],
         pltpu.with_memory_space_constraint(nullspace, pltpu.HBM), pltpu.with_memory_space_constraint(sent, pltpu.HBM),
         mib=4, place=pltpu.HBM,
     )

time: 54.5 us -> 54.5 us (level)
  no operation moved by 1% of the time
where the time goes in v5:
time: 54.5 us; the launch traced here: 54.1 us
  starting transfers between devices  21.3 us (39%)
  waiting for transfers between devices  19.9 us (37%)
  Pallas kernels  11.5 us (21%)
  between operations  0.75 us (1%)
  local copies, waits for them, and re-layouts  0.7 us (1%)
    all_to_all x2, starting transfers between devices, exchange(): return lax.all_to_all(message, AXES, 0, 0, tiled=True)  21.3 us
    all_to_all x2, waiting for transfers between devices, exchange(): return lax.all_to_all(message, AXES, 0, 0, tiled=True)  19.9 us
    pallas_call x5, Pallas kernels, call(): pl.pallas_call(kernel, out_shape=out_shape, in_specs=specs, out_specs=tup...  11.5 us
  transfers between devices with their start and end apart: 2, of which 2 were waited for; matrix products, arithmetic and copies ran while one was open for 0% of the time, Pallas kernels for 10%

profile of v5, /device:TPU:1, one launch (start us, length us, event | category | flops | bytes accessed | tf_op | source)
XLA Modules:
  0.0 54.1 jit_solution(18292962896042309402)
XLA Ops:
  0.6 2.5 %pick_kernel.1 = f32[256,128]{1,0:T(8,128)} custom-call(f32[6,4608]{1,0:T(8,128)} %rows_ref.3, s32[18,1,256]{2,1,0:T(1,128)} %bitcast.16), custom_call_target="tpu_custom_call" | custom-call | tf_op jit(solution)/shard_map/pick_kernel/pallas_call | solution.py:279
  3.2 0.0 copy-start
  3.2 0.0 copy-start.2
  3.2 0.0 copy-start.3
  3.2 0.0 copy-start.4
  3.2 15.7 %all-to-all-start = ((f32[256,1,128]{2,1,0:T(1,128)}), f32[256,1,128]{2,1,0:T(1,128)S(1)}, u32[]{:S(2)}, u32[]{:S(2)}) async-start(f32[256,1,128]{2,1,0:T(1,128)} %bitcast.2), calls=%async_computation | async-start | bytes 262144 | tf_op jit(solution)/shard_map/all_to_all | solution.py:291
  18.9 0.0 copy-start.1
  18.9 0.0 copy-done
  18.9 0.0 copy-done.2
  18.9 0.0 copy-done.3
  18.9 0.0 copy-done.4
  18.9 0.7 %copy-done.1 = s32[1,256,18]{1,0,2:T(1,128)S(1)} copy-done((s32[1,256,18]{1,0,2:T(1,128)S(1)}, s32[1,256,18]{1,0,2:T(1,128)}, u32[]{:S(2)}) %copy-start.1) | copy-done | bytes 18456
  19.6 1.2 %own_kernel.1 = (f32[32,64]{1,0:T(8,128)S(1)}, s32[36,128]{1,0:T(8,128)S(1)}, bf16[64,4608]{1,0:T(8,128)(2,1)S(1)}, bf16[64,4608]{1,0:T(8,128)(2,1)S(1)}, s32[36,128]{1,0:T(8,128)S(1)}) custom-call(s32[1]{0:T(128)} %bitcast.4.me_ref, f32[6,4608]{1,0:T(8,128)S(1)} %copy-done, s32[36,128]{1,0:T(8,128)S(1)} %bitcast.20, s32[36,128]{1,0:T(8,128)S(1)} %bitcast.21, ...), custom_call_target="tpu_custom_call" | custom-call | tf_op jit(solution)/shard_map/own_kernel/pallas_call | solution.py:279
  20.8 11.1 %all-to-all-done = f32[256,1,128]{2,1,0:T(1,128)S(1)} async-done(((f32[256,1,128]{2,1,0:T(1,128)}), f32[256,1,128]{2,1,0:T(1,128)S(1)}, u32[]{:S(2)}, u32[]{:S(2)}) %all-to-all-start) | async-done | bytes 131104 | tf_op jit(solution)/shard_map/all_to_all | solution.py:291
  31.9 1.9 %factor_kernel.1 = (f32[256,128]{1,0:T(8,128)}, f32[36,64]{1,0:T(8,128)}, f32[48,64]{1,0:T(8,128)S(1)}, f32[8,4608]{1,0:T(8,128)S(1)}) custom-call(f32[256,128]{1,0:T(8,128)S(1)} %bitcast.15, bf16[64,4608]{1,0:T(8,128)(2,1)S(1)} %get-tuple-element.14.landed_ref, f32[32,64]{1,0:T(8,128)S(1)} %get-tuple-element.15.gram_ref), custom_call_target="tpu_custom_call" | custom-call | tf_op jit(solution)/shard_map/factor_kernel/pallas_call | solution.py:279
  33.7 0.0 copy-start.5
  33.7 5.7 %all-to-all-start.1 = ((f32[256,1,128]{2,1,0:T(1,128)}), f32[256,1,128]{2,1,0:T(1,128)S(1)}, u32[]{:S(2)}, u32[]{:S(2)}) async-start(f32[256,1,128]{2,1,0:T(1,128)} %bitcast.9), calls=%async_computation.1 | async-start | bytes 262144 | tf_op jit(solution)/shard_map/all_to_all | solution.py:291
  39.4 0.0 copy-done.5
  39.4 4.3 %padded_kernel.1 = (f32[6,8192]{1,0:T(8,128)}, f32[8,4608]{1,0:T(8,128)S(1)}) custom-call(f32[6,4608]{1,0:T(8,128)S(1)} %copy-done, s32[36,128]{1,0:T(8,128)S(1)} %get-tuple-element.18.agg_ref, s32[36,128]{1,0:T(8,128)S(1)} %bitcast.22, s32[18,1,256]{2,1,0:T(1,128)S(1)} %bitcast.19, f32[48,64]{1,0:T(8,128)S(1)} %get-tuple-element.19.table_ref, ...), custom_call_target="tpu_custom_call" | custom-call | tf_op jit(solution)/shard_map/padded_kernel/pallas_call | solution.py:279
  43.7 8.8 %all-to-all-done.1 = f32[256,1,128]{2,1,0:T(1,128)S(1)} async-done(((f32[256,1,128]{2,1,0:T(1,128)}), f32[256,1,128]{2,1,0:T(1,128)S(1)}, u32[]{:S(2)}, u32[]{:S(2)}) %all-to-all-start.1) | async-done | bytes 131104 | tf_op jit(solution)/shard_map/all_to_all | solution.py:291
  52.5 1.6 %fine_kernel.1 = f32[6,4608]{1,0:T(8,128)} custom-call(f32[256,128]{1,0:T(8,128)S(1)} %bitcast.14, s32[36,128]{1,0:T(8,128)S(1)} %get-tuple-element.17.source_ref, f32[8,4608]{1,0:T(8,128)S(1)} %get-tuple-element.22.own_ref), custom_call_target="tpu_custom_call" | custom-call | tf_op jit(solution)/shard_map/fine_kernel/pallas_call | solution.py:279
Async XLA Ops:
  3.2 15.7 %copy-start = (f32[6,4608]{1,0:T(8,128)S(1)}, f32[6,4608]{1,0:T(8,128)}, u32[]{:S(2)}) copy-start(f32[6,4608]{1,0:T(8,128)} %rows_ref.3) | copy-start | bytes 331780
  3.2 15.7 %copy-start.2 = (s32[1,256,18]{1,0,2:T(1,128)S(1)}, s32[1,256,18]{1,0,2:T(1,128)}, u32[]{:S(2)}) copy-start(s32[1,256,18]{1,0,2:T(1,128)} %param.11) | copy-start | bytes 55300
  3.2 15.7 %copy-start.3 = (s32[4608]{0:T(1024)S(1)}, s32[4608]{0:T(1024)}, u32[]{:S(2)}) copy-start(s32[4608]{0:T(1024)} %param.7) | copy-start | bytes 55300
  3.2 15.7 %copy-start.4 = (s32[4608]{0:T(1024)S(1)}, s32[4608]{0:T(1024)}, u32[]{:S(2)}) copy-start(s32[4608]{0:T(1024)} %param.8) | copy-start | bytes 55300
  3.2 28.6 %all-to-all-start = ((f32[256,1,128]{2,1,0:T(1,128)}), f32[256,1,128]{2,1,0:T(1,128)S(1)}, u32[]{:S(2)}, u32[]{:S(2)}) async-start(f32[256,1,128]{2,1,0:T(1,128)} %bitcast.2), calls=%async_computation | async-start | bytes 262144 | tf_op jit(solution)/shard_map/all_to_all | solution.py:291
  18.9 0.7 %copy-start.1 = (s32[1,256,18]{1,0,2:T(1,128)S(1)}, s32[1,256,18]{1,0,2:T(1,128)}, u32[]{:S(2)}) copy-start(s32[1,256,18]{1,0,2:T(1,128)} %param.10) | copy-start | bytes 55300
  33.7 5.7 %copy-start.5 = (s32[4608]{0:T(1024)S(1)}, s32[4608]{0:T(1024)}, u32[]{:S(2)}) copy-start(s32[4608]{0:T(1024)} %param.9) | copy-start | bytes 55300
  33.7 18.8 %all-to-all-start.1 = ((f32[256,1,128]{2,1,0:T(1,128)}), f32[256,1,128]{2,1,0:T(1,128)S(1)}, u32[]{:S(2)}, u32[]{:S(2)}) async-start(f32[256,1,128]{2,1,0:T(1,128)} %bitcast.9), calls=%async_computation.1 | async-start | bytes 262144 | tf_op jit(solution)/shard_map/all_to_all | solution.py:291
